TPU v7x, 512 devices: a whole 4x4x16 slice. The times are simulated.
512 devices in a mesh: chol: 16 (over z_lo, core), walk: 32 (over y, x, z_hi).
Axes of the slice: x: 4, y: 4, z: 16 (z_hi: 2, z_lo: 8; z = z_hi * 8 + z_lo), core: 2. Of those that a mesh axis runs over, the one named last changes fastest.
Arguments:
- orbitals: float32 [32, 1024, 200], P('walk', 'chol'), may hold values from -6 to 6
- inverse_intersection: float32 [32, 200, 200], P('walk'), may hold values from -0.4375 to 0.4375
- half_rotated: bfloat16 [16, 200, 1024], P('chol'), may hold values from -0.013671875 to 0.013671875
- chol_full: bfloat16 [16, 1024, 1024], P('chol', 'walk'), as said below
- fields: float32 [16, 32], P('chol', 'walk'), may hold values from -6 to 6
Outputs:
- orbitals_next: float32 [32, 1024, 200], P('walk', 'chol')
Inputs may be any that keep to these rules, and one draw needn't show every extreme that they name: Every 1024 x 1024 matrix chol_full[g] is symmetric.
All inputs are finite; a program needn't handle non-finite values.
Results may differ from a plain program's by a relative error of at most 0.0041.
Values may be sent and summed in bfloat16 or wider, within the bound.
No kernel may reach another device: no remote copies, remote signals or barrier semaphores. Data moves between devices by JAX's collectives and lax.ppermute only.
A program may use at most 64 MiB of HBM per device.

v0:
```python
import jax
import jax.numpy as jnp
from jax import lax
from jax.sharding import PartitionSpec as P

TAYLOR = 5


field_scale = 0.4


def shards(orbitals, inverse_intersection, half_rotated, chol_full, fields):
    highest = lax.Precision.HIGHEST
    rows_here = orbitals.shape[1]
    basis = half_rotated.shape[2]
    theta_rows = jnp.einsum(
        "wno,wop->wnp", orbitals, inverse_intersection, precision=highest
    ).astype(jnp.bfloat16)
    orbitals_low = orbitals.astype(jnp.bfloat16)
    taylor_term = lax.all_gather(orbitals_low, "chol", axis=1, tiled=True)
    raw_bias = jnp.einsum(
        "gon,wno->gw",
        half_rotated,
        lax.all_gather(theta_rows, "chol", axis=1, tiled=True),
        preferred_element_type=jnp.float32,
    )
    shifted = field_scale * (fields - jnp.clip(raw_bias, -1.0, 1.0))
    result = orbitals
    vectors = lax.all_gather(chol_full, "walk", axis=1, tiled=True)

    def add_vector(index, running):
        weights = shifted[index]
        return running + weights[:, None, None] * vectors[index].astype(jnp.float32)[None]

    operator_zero = jnp.zeros((shifted.shape[1], basis, basis), jnp.float32)
    local_operator = lax.fori_loop(0, vectors.shape[0], add_vector, operator_zero)
    own_start = lax.axis_index("chol") * rows_here
    for degree in range(1, TAYLOR + 1):
        partial_value = jnp.einsum(
            "wmn,wno->wmo", local_operator, taylor_term.astype(jnp.float32), precision=highest
        )
        summed = lax.psum(partial_value, "chol")
        result = result + lax.dynamic_slice_in_dim(summed, own_start, rows_here, 1) / degree
        taylor_term = (summed / degree).astype(jnp.bfloat16)
    return result


def solution(mesh):
    return jax.shard_map(
        shards,
        mesh=mesh,
        in_specs=(
            P("walk", "chol", None),
            P("walk", None, None),
            P("chol", None, None),
            P("chol", "walk", None),
            P("chol", "walk"),
        ),
        out_specs=P("walk", "chol", None),
        check_vma=False,
    )
```

profile of v0, /device:TPU:1, one launch (start us, length us, event | category | flops | bytes accessed | tf_op | source)
XLA Modules:
  0.0 1163.7 jit_solution(197525427345246126)
XLA Ops:
  6.5 0.7 all-gather.3.cloned.1.call-update
  7.3 0.8 convert_element_type.34
  8.2 1.1 convolution_convert_fusion
  9.2 40.8 %all-gather = bf16[1024,200]{1,0:T(8,128)(2,1)S(1)} all-gather(bf16[64,200]{1,0:T(8,128)(2,1)S(1)} %convolution_convert_fusion), channel_id=2, replica_groups=mesh['chol'=16,'walk'=32] {'chol'}, dimensions={0}, use_global_device_ids=true | all-gather | bytes 435200 | tf_op jit(solution)/shard_map/all_gather | solution.py:24
  50.0 0.2 copy.12
  50.9 0.8 multiply_reduce_fusion
  52.4 29.7 %all_gather.11 = bf16[1,1024,200]{2,1,0:T(8,128)(2,1)S(1)} all-gather(bf16[1,64,200]{2,1,0:T(8,128)(2,1)S(1)} %convert_element_type.34), channel_id=1, replica_groups=mesh['chol'=16,'walk'=32] {'chol'}, dimensions={1}, use_global_device_ids=true | all-gather | bytes 435200 | tf_op jit(solution)/shard_map/all_gather | solution.py:20
  82.1 66.6 %all-gather.3.cloned.1.call-done = bf16[1,1024,1024]{2,1,0:T(8,128)(2,1)} async-done(((bf16[1,32,1024]{2,1,0:T(8,128)(2,1)}), bf16[1,1024,1024]{2,1,0:T(8,128)(2,1)}) %all-gather.3.cloned.1.call-update) | async-done | bytes 2097168 | tf_op jit(solution)/shard_map/all_gather | solution.py:29
  148.7 5.4 fusion.15
  154.1 0.0 all-reduce.8.cloned.1.call-start
  154.1 186.3 %all-reduce.6.cloned.1.call-done = f32[1,1024,200]{1,2,0:T(8,128)} async-done(((f32[1,1024,200]{1,2,0:T(8,128)}), f32[1,1024,200]{1,2,0:T(8,128)}) %all-reduce.6.cloned.1.call-update) | async-done | bytes 819216 | tf_op jit(solution)/shard_map/psum | solution.py:42
  340.5 4.6 fusion.18
  345.2 0.0 all-reduce.10.cloned.1.call-start
  345.2 198.8 %all-reduce.8.cloned.1.call-done = f32[1,1024,200]{1,2,0:T(8,128)} async-done(((f32[1,1024,200]{1,2,0:T(8,128)}), f32[1,1024,200]{1,2,0:T(8,128)}) %all-reduce.8.cloned.1.call-update) | async-done | bytes 819216 | tf_op jit(solution)/shard_map/psum | solution.py:42
  544.1 4.7 fusion.21
  548.8 198.9 %all-reduce.10.cloned.1.call-done = f32[1,1024,200]{1,2,0:T(8,128)} async-done(((f32[1,1024,200]{1,2,0:T(8,128)}), f32[1,1024,200]{1,2,0:T(8,128)}) %all-reduce.10.cloned.1.call-update) | async-done | bytes 819216 | tf_op jit(solution)/shard_map/psum | solution.py:42
  747.7 4.7 fusion.24
  752.4 0.2 all-reduce.14.cloned.1.call-start
  752.7 198.6 %all-reduce.12.cloned.1.call-done = f32[1,1024,200]{1,2,0:T(8,128)} async-done(((f32[1,1024,200]{1,2,0:T(8,128)}), f32[1,1024,200]{1,2,0:T(8,128)}) %all-reduce.12.cloned.1.call-update) | async-done | bytes 819216 | tf_op jit(solution)/shard_map/psum | solution.py:42
  951.3 4.7 fusion.27
  956.0 0.1 copy.6
  956.1 198.8 %all-reduce.14.cloned.1.call-done = f32[1,1024,200]{1,2,0:T(8,128)} async-done(((f32[1,1024,200]{1,2,0:T(8,128)}), f32[1,1024,200]{1,2,0:T(8,128)}) %all-reduce.14.cloned.1.call-update) | async-done | bytes 819216 | tf_op jit(solution)/shard_map/psum | solution.py:42
  1154.9 1.3 multiply_add_fusion
  1156.2 0.7 copy.7
  (16 shorter events, 0.2 us)
Async XLA Ops:
  6.5 1.6 copy-start
  6.5 44.3 %copy-start.3 = (bf16[1,200,1024]{2,1,0:T(8,128)(2,1)S(1)}, bf16[1,200,1024]{2,1,0:T(8,128)(2,1)}, u32[]{:S(2)}) copy-start(bf16[1,200,1024]{2,1,0:T(8,128)(2,1)} %param.7) | copy-start | bytes 1228804
  6.5 142.1 %all-gather.3.cloned.1.call-start = ((), (), s32[]{:S(2)}) async-start(), calls=%async_computation | async-start | bytes 2162688 | tf_op jit(solution)/shard_map/all_gather | solution.py:29
  7.3 333.2 %all-reduce.6.cloned.1.call-start = ((), (), s32[]{:S(2)}) async-start(), calls=%async_computation.1 | async-start | bytes 1638400 | tf_op jit(solution)/shard_map/psum | solution.py:42
  148.7 191.8 %copy-start.1 = (bf16[1,1024,1024]{2,1,0:T(8,128)(2,1)S(1)}, bf16[1,1024,1024]{2,1,0:T(8,128)(2,1)}, u32[]{:S(2)}) copy-start(bf16[1,1024,1024]{2,1,0:T(8,128)(2,1)} %all-gather.3.cloned.1.call-done) | copy-start | bytes 6291460
  154.1 390.0 %all-reduce.8.cloned.1.call-start = ((), (), s32[]{:S(2)}) async-start(), calls=%async_computation.2 | async-start | bytes 1638400 | tf_op jit(solution)/shard_map/psum | solution.py:42
  345.2 402.5 %all-reduce.10.cloned.1.call-start = ((), (), s32[]{:S(2)}) async-start(), calls=%async_computation.3 | async-start | bytes 1638400 | tf_op jit(solution)/shard_map/psum | solution.py:42
  548.8 402.5 %all-reduce.12.cloned.1.call-start = ((), (), s32[]{:S(2)}) async-start(), calls=%async_computation.4 | async-start | bytes 1638400 | tf_op jit(solution)/shard_map/psum | solution.py:42
  752.4 203.6 %copy-start.2 = (f32[1,64,200]{2,1,0:T(8,128)S(1)}, f32[1,64,200]{2,1,0:T(8,128)}, u32[]{:S(2)}) copy-start(f32[1,64,200]{2,1,0:T(8,128)} %param.5) | copy-start | bytes 153604
  752.4 402.5 %all-reduce.14.cloned.1.call-start = ((), (), s32[]{:S(2)}) async-start(), calls=%async_computation.5 | async-start | bytes 1638400 | tf_op jit(solution)/shard_map/psum | solution.py:42
Sparse Core Ops, SparseCore 0:
  11.7 136.9 all-gather.2
  154.2 186.2 all-reduce.5
  345.3 198.7 all-reduce.7
  548.9 198.7 all-reduce.9
  752.5 198.6 all-reduce.11
  956.1 198.7 all-reduce.13
where the time goes:
time: 1170 us; the launch traced here: 1160 us
  waiting for transfers between devices  1050 us (90%)
  blocking collectives  70.5 us (6%)
  matrix products  25.2 us (2%)
  between operations  14.8 us (1%)
    psum x5, waiting for transfers between devices, shards(): summed = lax.psum(partial_value, 'chol')  981 us
    all_gather x1, waiting for transfers between devices, shards(): vectors = lax.all_gather(chol_full, 'walk', axis=1, tiled=True)  66.6 us
    all_gather x1, blocking collectives, shards(): lax.all_gather(theta_rows, 'chol', axis=1, tiled=True)  40.8 us
    all_gather x1, blocking collectives, shards(): taylor_term = lax.all_gather(orbitals_low, 'chol', axis=1, tiled=True)  29.7 us
    dot_general x5, matrix products, shards(): jnp.einsum('wmn,wno->wmo', local_operator, taylor_term.astype(jnp.float32...  24.1 us
  transfers between devices with their start and end apart: 6, of which 6 were waited for; matrix products, arithmetic and copies ran while one was open for 0% of the time, Pallas kernels for 0%

commit v1 on v0

v1 whole, which is shorter than its diff:
```python
import jax
import jax.numpy as jnp
from jax import lax
from jax.experimental import pallas as pl
from jax.experimental.pallas import tpu as pltpu
from jax.sharding import Mesh, PartitionSpec as P

TAYLOR = 5
field_scale = 0.4
f32, bf16 = jnp.float32, jnp.bfloat16

CHOL = ("zl", "core")
WALK = ("y", "x", "zh")
PLANE = ("y", "x")
HIGHEST = lax.Precision.HIGHEST
NT = (((1,), (1,)), ((), ()))


def iota(shape, dim):
    return lax.broadcasted_iota(jnp.int32, shape, dim)


def plane_index():
    return lax.axis_index("y") * 4 + lax.axis_index("x")


def chol_index():
    return lax.axis_index("zl") * 2 + lax.axis_index("core")


def first_kernel(orb_ref, inv_ref, hr_ref, chol_ref, theta_ref, hrc_ref, piece_ref, low_ref, rows_lo, rows_hi):
    p = plane_index()
    start = p // 2
    for d in range(5):
        col = pl.multiple_of(lax.rem(start + d, 8) * 128, 128)
        piece_ref[:, 128 * d:128 * d + 128] = chol_ref[:, pl.ds(col, 128)]
    rows_lo[...] = jnp.zeros_like(rows_lo)
    rows_hi[...] = jnp.zeros_like(rows_hi)
    for i in range(13):
        @pl.when(p == i)
        def _():
            if i < 12:
                both = hr_ref[16 * i:16 * i + 16, :].astype(f32)
                rows_lo[...] = both[0:8]
                rows_hi[...] = both[8:16]
            else:
                rows_lo[...] = hr_ref[192:200, :].astype(f32)
    left = iota((8, 128), 1) < 64
    for u in range(8):
        low = rows_lo[:, 128 * u:128 * u + 128]
        high = rows_hi[:, 128 * u:128 * u + 128]
        hrc_ref[2 * u] = jnp.where(left, low, pltpu.roll(high, 64, 1)).astype(bf16)
        hrc_ref[2 * u + 1] = jnp.where(left, pltpu.roll(low, 64, 1), high).astype(bf16)
    orb = orb_ref[...]
    twice = jnp.concatenate([orb, orb], axis=0)
    theta_t = lax.dot_general(inv_ref[...], twice, (((0,), (1,)), ((), ())), precision=HIGHEST,
                              preferred_element_type=f32)
    for i in range(16):
        if i < 12:
            tile = jnp.where(left, theta_t[16 * i:16 * i + 8], theta_t[16 * i + 8:16 * i + 16])
        elif i == 12:
            tile = jnp.where(left, theta_t[192:200], 0.0)
        else:
            tile = jnp.zeros((8, 128), f32)
        theta_ref[i] = tile.astype(bf16)
    low_ref[...] = jnp.concatenate([orb, jnp.zeros((64, 56), f32)], axis=1).astype(bf16)


def bias_kernel(field_ref, hr_ref, theta_ref, out_ref):
    p = plane_index()
    h = hr_ref[...].astype(f32).reshape(128, 128).astype(bf16)
    t = theta_ref[...].astype(f32).reshape(128, 128).astype(bf16)
    pairs = lax.dot_general(h, t, NT, preferred_element_type=f32)
    row, col = iota((128, 128), 0), iota((128, 128), 1)
    pairs = jnp.where((row & 7) == (col & 7), pairs, 0.0)
    by_vector = pairs.reshape(16, 8, 128).sum(axis=1)
    gather = jnp.where((row >> 3) == col, 1.0, 0.0).astype(f32)
    part = jnp.dot(by_vector, gather, precision=HIGHEST, preferred_element_type=f32)
    tile = part + jnp.where(iota((16, 128), 1) == 16 + p, field_ref[0, 0], 0.0)
    for j in range(16):
        out_ref[j] = tile


def plane_sum_kernel(in_ref, out_ref):
    total = jnp.sum(in_ref[...], axis=0)
    row, col = iota((16, 128), 0), iota((16, 128), 1)
    tile = jnp.where((col < 16) | (row == chol_index()), total, 0.0)
    for j in range(16):
        out_ref[j] = tile


def operator_kernel(in_ref, near_ref, far_ref, out_ref):
    base = lax.axis_index("zl") * 2 + lax.axis_index("zh")
    total = jnp.sum(in_ref[...], axis=0)
    fields = pltpu.roll(total, 112, 1)
    shifted = field_scale * (fields - jnp.clip(total, -1.0, 1.0))
    shifted = jnp.where(iota((16, 128), 1) < 16, shifted, 0.0)
    by_walker = jnp.concatenate([shifted, jnp.zeros((112, 128), f32)], axis=0).T
    high = by_walker.astype(bf16)
    rest = (by_walker - high.astype(f32)).astype(bf16)
    g, q = iota((128, 512), 0), iota((128, 512), 1) >> 5
    j = q >> 1
    code = ((j & 1) << 3) | ((j & 2) << 1) | ((j & 4) >> 1) | (q & 1)
    pick = jnp.where(g == (code ^ base), 1.0, 0.0).astype(bf16)
    walkers = jnp.where((iota((512, 128), 0) >> 5) == iota((512, 128), 1), 1.0, 0.0).astype(bf16)
    same = (iota((512, 512), 0) & 31) == (iota((512, 512), 1) & 31)

    def weights(part):
        spread = jnp.dot(part, pick, preferred_element_type=f32).astype(bf16)
        full = jnp.dot(walkers, spread, preferred_element_type=f32)
        return jnp.where(same, full, 0.0).astype(bf16)

    w_high, w_rest = weights(high), weights(rest)
    near, far = near_ref[:, 0:640], far_ref[:, 0:640]
    for i in range(2):
        rows = slice(256 * i, 256 * i + 256)
        value = jnp.dot(w_rest[rows, :256], near, preferred_element_type=f32)
        value += jnp.dot(w_rest[rows, 256:], far, preferred_element_type=f32)
        value += jnp.dot(w_high[rows, :256], near, preferred_element_type=f32)
        value += jnp.dot(w_high[rows, 256:], far, preferred_element_type=f32)
        out_ref[rows, :] = value.astype(bf16)


def taylor_kernel(orb_ref, mine_ref, other_ref, low_mine_ref, low_other_ref, out_ref, op, term_a, term_b):
    z, k = lax.axis_index("zl"), lax.axis_index("core")
    order = (0, 4, 2, 6, 1, 5, 3, 7)
    for j in range(8):
        block = 2 * (z ^ order[j])
        here = pl.multiple_of((block + k) * 64, 64)
        there = pl.multiple_of((block + 1 - k) * 64, 64)
        term_a[pl.ds(here, 64), :] = low_mine_ref[64 * j:64 * j + 64, :]
        term_a[pl.ds(there, 64), :] = low_other_ref[64 * j:64 * j + 64, :]
    for p in range(16):
        here = pl.multiple_of(64 * p + 32 * k, 32)
        there = pl.multiple_of(64 * p + 32 * (1 - k), 32)
        for d in range(5):
            col = ((p // 2 + d) % 8) * 128
            op[pl.ds(here, 32), col:col + 128] = mine_ref[p, :, 128 * d:128 * d + 128]
            op[pl.ds(there, 32), col:col + 128] = other_ref[p, :, 128 * d:128 * d + 128]
    for i in range(8):
        for d in range(1, 4):
            j = (i + d) % 8
            block = op[128 * i:128 * i + 128, 128 * j:128 * j + 128].astype(f32)
            op[128 * j:128 * j + 128, 128 * i:128 * i + 128] = block.T.astype(bf16)
    own = pl.multiple_of((2 * z + k) * 64, 64)
    own_rows = op[pl.ds(own, 64), :]
    total = jnp.zeros((64, 256), f32)
    now, later = term_a, term_b
    for degree in range(1, TAYLOR + 1):
        term = now[...]
        total += jnp.dot(own_rows, term, preferred_element_type=f32) * (1.0 / degree)
        if degree < TAYLOR:
            for i in range(4):
                image = jnp.dot(op[256 * i:256 * i + 256, :], term, preferred_element_type=f32)
                later[256 * i:256 * i + 256, :] = (image * (1.0 / degree)).astype(bf16)
            now, later = later, now
    out_ref[...] = orb_ref[...] + total[:, :200]


def call(body, outs, *args, scratch=(), smem=0):
    vmem = pl.BlockSpec(memory_space=pltpu.VMEM)
    specs = [pl.BlockSpec(memory_space=pltpu.SMEM)] * smem + [vmem] * (len(args) - smem)
    many = isinstance(outs, (list, tuple))
    return pl.pallas_call(
        body,
        out_shape=outs,
        in_specs=specs,
        out_specs=[vmem] * len(outs) if many else vmem,
        scratch_shapes=list(scratch),
        compiler_params=pltpu.CompilerParams(vmem_limit_bytes=40 * 2**20),
    )(*args)


def shape(dims, dtype):
    return jax.ShapeDtypeStruct(dims, dtype)


def exchange(value, axes):
    return lax.all_to_all(value, axes, 0, 0, tiled=True)


def shards(orbitals, inverse_intersection, half_rotated, chol_full, fields):
    orb = orbitals[0]
    theta, hr_cut, piece, low = call(
        first_kernel,
        [shape((16, 8, 128), bf16), shape((16, 8, 128), bf16), shape((32, 640), bf16), shape((64, 256), bf16)],
        orb, inverse_intersection[0], half_rotated[0], chol_full[0],
        scratch=[pltpu.VMEM((8, 1024), f32), pltpu.VMEM((8, 1024), f32)],
    )
    pairs = [(k * 2 + h, h * 2 + k) for k in range(2) for h in range(2)]
    cross = [(k * 2 + h, h * 2 + 1 - k) for k in range(2) for h in range(2)]
    straight = lax.ppermute(piece, ("core", "zh"), pairs)
    crossed = lax.ppermute(piece, ("core", "zh"), cross)
    hr_all = exchange(hr_cut, CHOL)
    held = jnp.concatenate([jnp.concatenate([straight, crossed], axis=0), low], axis=1)

    def swap(value, bit):
        return lax.ppermute(value, "zl", [(i, i ^ bit) for i in range(8)])

    theta_all = exchange(theta, PLANE)
    held = jnp.concatenate([held, swap(held, 4)], axis=0)
    partial = call(bias_kernel, shape((16, 16, 128), f32), fields, hr_all, theta_all, smem=1)
    in_plane = exchange(partial, PLANE)
    held = jnp.concatenate([held, swap(held, 2)], axis=0)
    summed = call(plane_sum_kernel, shape((16, 16, 128), f32), in_plane)
    everywhere = exchange(summed, CHOL)
    far = swap(held, 1)
    lows = jnp.concatenate([held[:, 640:], far[:, 640:]], axis=0)
    swap_core = [(0, 1), (1, 0)]
    lows_other = lax.ppermute(lows, "core", swap_core)
    pieces = call(operator_kernel, shape((512, 640), bf16), everywhere, held, far)
    mine = exchange(pieces.reshape(16, 32, 640), PLANE)
    other = lax.ppermute(mine, "core", swap_core)
    out = call(
        taylor_kernel, shape((64, 200), f32), orb, mine, other, lows, lows_other,
        scratch=[pltpu.VMEM((1024, 1024), bf16), pltpu.VMEM((1024, 256), bf16), pltpu.VMEM((1024, 256), bf16)],
    )
    return out[None]


def solution(mesh):
    fine = Mesh(mesh.devices.reshape(8, 2, 4, 4, 2), ("zl", "core", "y", "x", "zh"))
    return jax.shard_map(
        shards,
        mesh=fine,
        in_specs=(
            P(WALK, CHOL, None),
            P(WALK, None, None),
            P(CHOL, None, None),
            P(CHOL, WALK, None),
            P(CHOL, WALK),
        ),
        out_specs=P(WALK, CHOL, None),
        check_vma=False,
    )
```

time: 1170 us -> 123 us (0.11)
  waiting for transfers between devices: 1050 us -> 23 us
  starting transfers between devices: 0.39 us -> 48 us
  blocking collectives: 70.5 us -> 37.1 us
  matrix products: 25.2 us -> 0 us
  between operations: 14.8 us -> 0.79 us
    psum x5 -> x0, waiting for transfers between devices: 981 us -> none  [shards(): summed = lax.psum(partial_value, 'chol')]
    all_gather x2 -> x0, blocking collectives: 70.5 us -> none  [the longest x1 40.8 us: shards(): lax.all_gather(theta_rows, 'chol', axis=1, tiled=True)]
    all_gather x1 -> x0, waiting for transfers between devices: 66.6 us -> none  [shards(): vectors = lax.all_gather(chol_full, 'walk', axis=1, tiled=True)]
    all_to_all x0 -> x3, blocking collectives: none -> 37.1 us  [exchange(): return lax.all_to_all(value, axes, 0, 0, tiled=True)]
    ppermute x0 -> x7, starting transfers between devices: none -> 36.3 us  [the longest x3 11.5 us: swap(): return lax.ppermute(value, 'zl', [(i, i ^ bit) for i in range(8)])]
    dot_general x6 -> x0, matrix products: 25.2 us -> none  [the longest x5 24.1 us: shards(): jnp.einsum('wmn,wno->wmo', local_operator, taylor_term.astype(jnp.float32...]
    all_to_all x0 -> x2, waiting for transfers between devices: none -> 14 us  [exchange(): return lax.all_to_all(value, axes, 0, 0, tiled=True)]
    all_to_all x0 -> x2, starting transfers between devices: none -> 11.8 us  [exchange(): return lax.all_to_all(value, axes, 0, 0, tiled=True)]
  transfers between devices with their start and end apart: 6 -> 9, of which waited for: 6 -> 5; matrix products, arithmetic and copies ran while one was open for 0% -> 0% of each run, Pallas kernels for 0% -> 1%
where the time goes in v1:
time: 123 us; the launch traced here: 121 us
  starting transfers between devices  48 us (39%)
  blocking collectives  37.1 us (30%)
  waiting for transfers between devices  23 us (19%)
  Pallas kernels  8.11 us (7%)
  local copies, waits for them, and re-layouts  3.64 us (3%)
    all_to_all x3, blocking collectives, exchange(): return lax.all_to_all(value, axes, 0, 0, tiled=True)  37.1 us
    all_to_all x2, waiting for transfers between devices, exchange(): return lax.all_to_all(value, axes, 0, 0, tiled=True)  14 us
    all_to_all x2, starting transfers between devices, exchange(): return lax.all_to_all(value, axes, 0, 0, tiled=True)  11.8 us
    ppermute x3, starting transfers between devices, swap(): return lax.ppermute(value, 'zl', [(i, i ^ bit) for i in range(8)])  11.5 us
    ppermute x1, starting transfers between devices, shards(): straight = lax.ppermute(piece, ('core', 'zh'), pairs)  9.97 us
    ppermute x1, starting transfers between devices, shards(): crossed = lax.ppermute(piece, ('core', 'zh'), cross)  8.77 us
    pallas_call x5, Pallas kernels, call(): pl.pallas_call(body, out_shape=outs, in_specs=specs, out_specs=[vmem] * l...  8.11 us
    ppermute x1, starting transfers between devices, shards(): other = lax.ppermute(mine, 'core', swap_core)  4.12 us
  transfers between devices with their start and end apart: 9, of which 5 were waited for; matrix products, arithmetic and copies ran while one was open for 0% of the time, Pallas kernels for 1%

profile of v1, /device:TPU:1, one launch (start us, length us, event | category | flops | bytes accessed | tf_op | source)
XLA Modules:
  0.0 120.8 jit_solution(3164097787742646979)
XLA Ops:
  0.0 1.0 copy-done
  1.0 0.8 copy-done.1
  1.8 0.9 copy-done.3
  2.8 0.8 copy-done.4
  3.6 1.0 shard_map.55
  4.6 8.8 %collective-permute-start.1 = (bf16[32,640]{1,0:T(8,128)(2,1)S(1)}, bf16[32,640]{1,0:T(8,128)(2,1)S(1)}, u32[]{:S(2)}, u32[]{:S(2)}) collective-permute-start(bf16[32,640]{1,0:T(8,128)(2,1)S(1)} %get-tuple-element.11), channel_id=1, source_target_pairs={{0,1},{1,33},{32,0},{33,32},{2,3},{3,35},{34,2},{35,34},{4,5},{5,3... | collective-permute-start | bytes 122888 | tf_op jit(solution)/shard_map/ppermute | solution.py:193
  13.4 10.0 %collective-permute-start = (bf16[32,640]{1,0:T(8,128)(2,1)S(1)}, bf16[32,640]{1,0:T(8,128)(2,1)S(1)}, u32[]{:S(2)}, u32[]{:S(2)}) collective-permute-start(bf16[32,640]{1,0:T(8,128)(2,1)S(1)} %get-tuple-element.11), channel_id=1, source_target_pairs={{0,0},{1,32},{32,1},{33,33},{2,2},{3,34},{34,3},{35,35},{4,4},{5,3... | collective-permute-start | bytes 122888 | tf_op jit(solution)/shard_map/ppermute | solution.py:192
  23.4 4.0 %collective-permute-done = bf16[32,640]{1,0:T(8,128)(2,1)S(1)} collective-permute-done((bf16[32,640]{1,0:T(8,128)(2,1)S(1)}, bf16[32,640]{1,0:T(8,128)(2,1)S(1)}, u32[]{:S(2)}, u32[]{:S(2)}) %collective-permute-start) | collective-permute-done | bytes 40992 | tf_op jit(solution)/shard_map/ppermute | solution.py:192
  27.4 4.0 %collective-permute-start.2 = (bf16[64,896]{1,0:T(8,128)(2,1)S(1)}, bf16[64,896]{1,0:T(8,128)(2,1)S(1)}, u32[]{:S(2)}, u32[]{:S(2)}) collective-permute-start(bf16[64,896]{1,0:T(8,128)(2,1)S(1)} %pad_maximum_fusion.3), channel_id=1, source_target_pairs={{0,256},{64,320},{128,384},{192,448},{256,0},{320,64},{384,128},{4... | collective-permute-start | bytes 344072 | tf_op jit(solution)/shard_map/ppermute | solution.py:198
  31.4 13.0 %all_to_all.25.theta_ref = bf16[16,8,128]{2,1,0:T(8,128)(2,1)S(1)} all-to-all(bf16[16,8,128]{2,1,0:T(8,128)(2,1)S(1)} %get-tuple-element.10), channel_id=1, replica_groups=mesh['zl'=8,'core'=2,'y'=4,'x'=4,'zh'=2] {'y','x'}, dimensions={0} | all-to-all | bytes 65536 | tf_op jit(solution)/shard_map/all_to_all | solution.py:179
  44.4 6.2 %all-to-all-start = ((bf16[16,8,128]{2,1,0:T(8,128)(2,1)}), bf16[16,8,128]{2,1,0:T(8,128)(2,1)S(1)}, u32[]{:S(2)}, u32[]{:S(2)}) async-start(bf16[16,8,128]{2,1,0:T(8,128)(2,1)} %get-tuple-element.9), calls=%async_computation | async-start | bytes 65536 | tf_op jit(solution)/shard_map/all_to_all | solution.py:179
  50.6 4.2 %collective-permute-start.3 = (bf16[128,896]{1,0:T(8,128)(2,1)S(1)}, bf16[128,896]{1,0:T(8,128)(2,1)S(1)}, u32[]{:S(2)}, u32[]{:S(2)}) collective-permute-start(bf16[128,896]{1,0:T(8,128)(2,1)S(1)} %pad_maximum_fusion.2), channel_id=1, source_target_pairs={{0,128},{64,192},{128,0},{192,64},{256,384},{320,448},{384,256},{4... | collective-permute-start | bytes 688136 | tf_op jit(solution)/shard_map/ppermute | solution.py:198
  55.5 5.0 %all-to-all-done.hr_ref = bf16[16,8,128]{2,1,0:T(8,128)(2,1)S(1)} async-done(((bf16[16,8,128]{2,1,0:T(8,128)(2,1)}), bf16[16,8,128]{2,1,0:T(8,128)(2,1)S(1)}, u32[]{:S(2)}, u32[]{:S(2)}) %all-to-all-start) | async-done | bytes 32800 | tf_op jit(solution)/shard_map/all_to_all | solution.py:179
  60.8 9.7 %all_to_all.26.in_ref = f32[16,16,128]{2,1,0:T(8,128)S(1)} all-to-all(f32[16,16,128]{2,1,0:T(8,128)S(1)} %shard_map.56), channel_id=1, replica_groups=mesh['zl'=8,'core'=2,'y'=4,'x'=4,'zh'=2] {'y','x'}, dimensions={0} | all-to-all | bytes 262144 | tf_op jit(solution)/shard_map/all_to_all | solution.py:179
  71.1 5.6 %all-to-all-start.3 = ((f32[16,16,128]{2,1,0:T(8,128)}), f32[16,16,128]{2,1,0:T(8,128)S(1)}, u32[]{:S(2)}, u32[]{:S(2)}) async-start(f32[16,16,128]{2,1,0:T(8,128)} %shard_map.57), calls=%async_computation.3 | async-start | bytes 262144 | tf_op jit(solution)/shard_map/all_to_all | solution.py:179
  76.8 3.3 %collective-permute-start.4 = (bf16[256,896]{1,0:T(8,128)(2,1)S(1)}, bf16[256,896]{1,0:T(8,128)(2,1)S(1)}, u32[]{:S(2)}, u32[]{:S(2)}) collective-permute-start(bf16[256,896]{1,0:T(8,128)(2,1)S(1)} %pad_maximum_fusion.near_ref), channel_id=1, source_target_pairs={{0,64},{64,0},{128,192},{192,128},{256,320},{320,256},{384,448},{4... | collective-permute-start | bytes 1376264 | tf_op jit(solution)/shard_map/ppermute | solution.py:198
  80.1 9.0 %all-to-all-done.3.in_ref = f32[16,16,128]{2,1,0:T(8,128)S(1)} async-done(((f32[16,16,128]{2,1,0:T(8,128)}), f32[16,16,128]{2,1,0:T(8,128)S(1)}, u32[]{:S(2)}, u32[]{:S(2)}) %all-to-all-start.3) | async-done | bytes 131104 | tf_op jit(solution)/shard_map/all_to_all | solution.py:179
  89.1 3.5 %collective-permute-done.4.far_ref = bf16[256,896]{1,0:T(8,128)(2,1)S(1)} collective-permute-done((bf16[256,896]{1,0:T(8,128)(2,1)S(1)}, bf16[256,896]{1,0:T(8,128)(2,1)S(1)}, u32[]{:S(2)}, u32[]{:S(2)}) %collective-permute-start.4) | collective-permute-done | bytes 458784 | tf_op jit(solution)/shard_map/ppermute | solution.py:198
  92.6 1.7 %shard_map.58 = bf16[512,640]{1,0:T(8,128)(2,1)S(1)} custom-call(f32[16,16,128]{2,1,0:T(8,128)S(1)} %all-to-all-done.3.in_ref, bf16[256,896]{1,0:T(8,128)(2,1)S(1)} %pad_maximum_fusion.near_ref, bf16[256,896]{1,0:T(8,128)(2,1)S(1)} %collective-permute-done.4.far_ref), custom_call_target="tpu_custom_call" | custom-call | tf_op jit(solution)/shard_map/pallas_call | solution.py:164
  94.3 14.5 %all_to_all.27.mine_ref = bf16[16,32,640]{2,1,0:T(8,128)(2,1)S(1)} all-to-all(bf16[16,32,640]{2,1,0:T(8,128)(2,1)S(1)} %bitcast.6), channel_id=1, replica_groups=mesh['zl'=8,'core'=2,'y'=4,'x'=4,'zh'=2] {'y','x'}, dimensions={0} | all-to-all | bytes 1310720 | tf_op jit(solution)/shard_map/all_to_all | solution.py:179
  108.8 4.1 %collective-permute-start.5 = (bf16[16,32,640]{2,1,0:T(8,128)(2,1)S(1)}, bf16[16,32,640]{2,1,0:T(8,128)(2,1)S(1)}, u32[]{:S(2)}, u32[]{:S(2)}) collective-permute-start(bf16[16,32,640]{2,1,0:T(8,128)(2,1)S(1)} %all_to_all.27.mine_ref), channel_id=1, source_target_pairs={{0,32},{32,0},{1,33},{33,1},{2,34},{34,2},{3,35},{35,3},{4,36},{36... | collective-permute-start | bytes 1966088 | tf_op jit(solution)/shard_map/ppermute | solution.py:213
  113.0 1.9 %collective-permute-start.6 = (bf16[512,256]{1,0:T(8,128)(2,1)S(1)}, bf16[512,256]{1,0:T(8,128)(2,1)S(1)}, u32[]{:S(2)}, u32[]{:S(2)}) collective-permute-start(bf16[512,256]{1,0:T(8,128)(2,1)S(1)} %pad_maximum_fusion.1.low_mine_ref), channel_id=1, source_target_pairs={{0,32},{32,0},{1,33},{33,1},{2,34},{34,2},{3,35},{35,3},{4,36},{36... | collective-permute-start | bytes 786440 | tf_op jit(solution)/shard_map/ppermute | solution.py:210
  114.9 1.5 %collective-permute-done.6.low_other_ref = bf16[512,256]{1,0:T(8,128)(2,1)S(1)} collective-permute-done((bf16[512,256]{1,0:T(8,128)(2,1)S(1)}, bf16[512,256]{1,0:T(8,128)(2,1)S(1)}, u32[]{:S(2)}, u32[]{:S(2)}) %collective-permute-start.6) | collective-permute-done | bytes 262176 | tf_op jit(solution)/shard_map/ppermute | solution.py:210
  116.4 4.4 %shard_map.59 = f32[64,200]{1,0:T(8,128)} custom-call(f32[64,200]{1,0:T(8,128)S(1)} %bitcast.9, bf16[16,32,640]{2,1,0:T(8,128)(2,1)S(1)} %all_to_all.27.mine_ref, bf16[16,32,640]{2,1,0:T(8,128)(2,1)S(1)} %collective-permute-done.5.other_ref, bf16[512,256]{1,0:T(8,128)(2,1)S(1)} %pad_maximum_fusion.1.low_mine_ref, ...), custom_call_target="tpu_custom_call" | custom-call | tf_op jit(solution)/shard_map/pallas_call | solution.py:164
  (18 shorter events, 1.2 us)
Async XLA Ops:
  0.0 1.0 copy-start
  1.0 0.8 copy-start.1
  1.8 0.9 copy-start.3
  2.8 0.8 copy-start.4
  4.6 18.8 %collective-permute-start.1 = (bf16[32,640]{1,0:T(8,128)(2,1)S(1)}, bf16[32,640]{1,0:T(8,128)(2,1)S(1)}, u32[]{:S(2)}, u32[]{:S(2)}) collective-permute-start(bf16[32,640]{1,0:T(8,128)(2,1)S(1)} %get-tuple-element.11), channel_id=1, source_target_pairs={{0,1},{1,33},{32,0},{33,32},{2,3},{3,35},{34,2},{35,34},{4,5},{5,3... | collective-permute-start | bytes 122888 | tf_op jit(solution)/shard_map/ppermute | solution.py:193
  13.4 14.0 %collective-permute-start = (bf16[32,640]{1,0:T(8,128)(2,1)S(1)}, bf16[32,640]{1,0:T(8,128)(2,1)S(1)}, u32[]{:S(2)}, u32[]{:S(2)}) collective-permute-start(bf16[32,640]{1,0:T(8,128)(2,1)S(1)} %get-tuple-element.11), channel_id=1, source_target_pairs={{0,0},{1,32},{32,1},{33,33},{2,2},{3,34},{34,3},{35,35},{4,4},{5,3... | collective-permute-start | bytes 122888 | tf_op jit(solution)/shard_map/ppermute | solution.py:192
  27.4 23.2 %collective-permute-start.2 = (bf16[64,896]{1,0:T(8,128)(2,1)S(1)}, bf16[64,896]{1,0:T(8,128)(2,1)S(1)}, u32[]{:S(2)}, u32[]{:S(2)}) collective-permute-start(bf16[64,896]{1,0:T(8,128)(2,1)S(1)} %pad_maximum_fusion.3), channel_id=1, source_target_pairs={{0,256},{64,320},{128,384},{192,448},{256,0},{320,64},{384,128},{4... | collective-permute-start | bytes 344072 | tf_op jit(solution)/shard_map/ppermute | solution.py:198
  44.4 16.0 %all-to-all-start = ((bf16[16,8,128]{2,1,0:T(8,128)(2,1)}), bf16[16,8,128]{2,1,0:T(8,128)(2,1)S(1)}, u32[]{:S(2)}, u32[]{:S(2)}) async-start(bf16[16,8,128]{2,1,0:T(8,128)(2,1)} %get-tuple-element.9), calls=%async_computation | async-start | bytes 65536 | tf_op jit(solution)/shard_map/all_to_all | solution.py:179
  50.6 26.1 %collective-permute-start.3 = (bf16[128,896]{1,0:T(8,128)(2,1)S(1)}, bf16[128,896]{1,0:T(8,128)(2,1)S(1)}, u32[]{:S(2)}, u32[]{:S(2)}) collective-permute-start(bf16[128,896]{1,0:T(8,128)(2,1)S(1)} %pad_maximum_fusion.2), channel_id=1, source_target_pairs={{0,128},{64,192},{128,0},{192,64},{256,384},{320,448},{384,256},{4... | collective-permute-start | bytes 688136 | tf_op jit(solution)/shard_map/ppermute | solution.py:198
  71.1 17.9 %all-to-all-start.3 = ((f32[16,16,128]{2,1,0:T(8,128)}), f32[16,16,128]{2,1,0:T(8,128)S(1)}, u32[]{:S(2)}, u32[]{:S(2)}) async-start(f32[16,16,128]{2,1,0:T(8,128)} %shard_map.57), calls=%async_computation.3 | async-start | bytes 262144 | tf_op jit(solution)/shard_map/all_to_all | solution.py:179
  76.8 15.8 %collective-permute-start.4 = (bf16[256,896]{1,0:T(8,128)(2,1)S(1)}, bf16[256,896]{1,0:T(8,128)(2,1)S(1)}, u32[]{:S(2)}, u32[]{:S(2)}) collective-permute-start(bf16[256,896]{1,0:T(8,128)(2,1)S(1)} %pad_maximum_fusion.near_ref), channel_id=1, source_target_pairs={{0,64},{64,0},{128,192},{192,128},{256,320},{320,256},{384,448},{4... | collective-permute-start | bytes 1376264 | tf_op jit(solution)/shard_map/ppermute | solution.py:198
  108.8 7.6 %collective-permute-start.5 = (bf16[16,32,640]{2,1,0:T(8,128)(2,1)S(1)}, bf16[16,32,640]{2,1,0:T(8,128)(2,1)S(1)}, u32[]{:S(2)}, u32[]{:S(2)}) collective-permute-start(bf16[16,32,640]{2,1,0:T(8,128)(2,1)S(1)} %all_to_all.27.mine_ref), channel_id=1, source_target_pairs={{0,32},{32,0},{1,33},{33,1},{2,34},{34,2},{3,35},{35,3},{4,36},{36... | collective-permute-start | bytes 1966088 | tf_op jit(solution)/shard_map/ppermute | solution.py:213
  112.9 3.5 %copy-start.2 = (f32[1,64,200]{2,1,0:T(8,128)S(1)}, f32[1,64,200]{2,1,0:T(8,128)}, u32[]{:S(2)}) copy-start(f32[1,64,200]{2,1,0:T(8,128)} %param.5) | copy-start | bytes 153604
  113.0 3.4 %collective-permute-start.6 = (bf16[512,256]{1,0:T(8,128)(2,1)S(1)}, bf16[512,256]{1,0:T(8,128)(2,1)S(1)}, u32[]{:S(2)}, u32[]{:S(2)}) collective-permute-start(bf16[512,256]{1,0:T(8,128)(2,1)S(1)} %pad_maximum_fusion.1.low_mine_ref), channel_id=1, source_target_pairs={{0,32},{32,0},{1,33},{33,1},{2,34},{34,2},{3,35},{35,3},{4,36},{36... | collective-permute-start | bytes 786440 | tf_op jit(solution)/shard_map/ppermute | solution.py:210

commit v2 on v1

v2 whole, which is shorter than its diff:
```python
import jax
import jax.numpy as jnp
from jax import lax
from jax.experimental import pallas as pl
from jax.experimental.pallas import tpu as pltpu
from jax.sharding import Mesh, PartitionSpec as P

TAYLOR = 5
field_scale = 0.4
f32, bf16 = jnp.float32, jnp.bfloat16

CHOL = ("zl", "core")
WALK = ("y", "x", "zh")
PLANE = ("y", "x")
HIGHEST = lax.Precision.HIGHEST
NT = (((1,), (1,)), ((), ()))


def iota(shape, dim):
    return lax.broadcasted_iota(jnp.int32, shape, dim)


def plane_index():
    return lax.axis_index("y") * 4 + lax.axis_index("x")


def chol_index():
    return lax.axis_index("zl") * 2 + lax.axis_index("core")


def first_kernel(field_ref, orb_hbm, inv_hbm, hr_hbm, chol_hbm, theta_ref, hrc_ref, piece_ref,
                 orb_ref, inv_ref, hr_ref, chol_ref, rows_lo, rows_hi, sems):
    pairs = ((chol_hbm, chol_ref), (hr_hbm, hr_ref), (orb_hbm, orb_ref), (inv_hbm, inv_ref))
    copies = [pltpu.make_async_copy(src, dst, sems.at[i]) for i, (src, dst) in enumerate(pairs)]
    for copy in copies:
        copy.start()
    p = plane_index()
    copies[0].wait()
    start = p // 2
    for d in range(5):
        col = pl.multiple_of(lax.rem(start + d, 8) * 128, 128)
        piece_ref[:, 128 * d:128 * d + 128] = chol_ref[:, pl.ds(col, 128)]
    rows_lo[...] = jnp.zeros_like(rows_lo)
    rows_hi[...] = jnp.zeros_like(rows_hi)
    copies[1].wait()
    for i in range(13):
        @pl.when(p == i)
        def _():
            if i < 12:
                both = hr_ref[16 * i:16 * i + 16, :].astype(f32)
                rows_lo[...] = both[0:8]
                rows_hi[...] = both[8:16]
            else:
                rows_lo[...] = hr_ref[192:200, :].astype(f32)
    left = iota((8, 128), 1) < 64
    for u in range(8):
        low = rows_lo[:, 128 * u:128 * u + 128]
        high = rows_hi[:, 128 * u:128 * u + 128]
        hrc_ref[2 * u] = jnp.where(left, low, pltpu.roll(high, 64, 1)).astype(bf16)
        hrc_ref[2 * u + 1] = jnp.where(left, pltpu.roll(low, 64, 1), high).astype(bf16)
    copies[2].wait()
    copies[3].wait()
    orb = orb_ref[...]
    twice = jnp.concatenate([orb, orb], axis=0)
    theta_t = lax.dot_general(inv_ref[...], twice, (((0,), (1,)), ((), ())), precision=HIGHEST,
                              preferred_element_type=f32)
    for i in range(13):
        if i < 12:
            tile = jnp.where(left, theta_t[16 * i:16 * i + 8], theta_t[16 * i + 8:16 * i + 16])
        else:
            tile = jnp.where(left, theta_t[192:200], 0.0)
        theta_ref[i] = tile.astype(bf16)
    field = jnp.full((8, 128), field_ref[0, 0], f32)
    high = field.astype(bf16).astype(f32)
    middle = (field - high).astype(bf16).astype(f32)
    row = iota((8, 128), 0)
    parts = jnp.where(row == 0, high, jnp.where(row == 1, middle, jnp.where(row == 2, field - high - middle, 0.0)))
    theta_ref[13] = parts.astype(bf16)


def spread_kernel(hr_ref, theta_ref, out_ref):
    for j in range(16):
        out_ref[j, 0:16] = hr_ref[...]
        out_ref[j, 16:30] = theta_ref[...]


def bias_kernel(in_ref, out_ref):
    pairs = jnp.zeros((128, 128), f32)
    for i in range(13):
        h = in_ref[i, 0:16].astype(f32).reshape(128, 128).astype(bf16)
        t = in_ref[:, 16 + i].astype(f32).reshape(128, 128).astype(bf16)
        pairs += lax.dot_general(h, t, NT, preferred_element_type=f32)
    row, col = iota((128, 128), 0), iota((128, 128), 1)
    pairs = jnp.where((row & 7) == (col & 7), pairs, 0.0)
    by_vector = pairs.reshape(16, 8, 128).sum(axis=1)
    gather = jnp.where((row >> 3) == col, 1.0, 0.0).astype(f32)
    part = jnp.dot(by_vector, gather, precision=HIGHEST, preferred_element_type=f32)
    fields = in_ref[:, 29].astype(f32).sum(axis=1)
    row, col = iota((16, 128), 0), iota((16, 128), 1)
    fields = jnp.sum(jnp.where(col == row + 16, fields, 0.0), axis=0, keepdims=True)
    tile = part + jnp.where(row == chol_index(), fields, 0.0)
    for j in range(16):
        out_ref[j] = tile


def operator_kernel(in_ref, held_ref, one_ref, two_ref, three_ref, out_ref):
    base = lax.axis_index("zl") * 2 + lax.axis_index("zh")
    total = jnp.sum(in_ref[...], axis=0)
    fields = pltpu.roll(total, 112, 1)
    shifted = field_scale * (fields - jnp.clip(total, -1.0, 1.0))
    shifted = jnp.where(iota((16, 128), 1) < 16, shifted, 0.0)
    by_walker = jnp.concatenate([shifted, jnp.zeros((112, 128), f32)], axis=0).T
    high = by_walker.astype(bf16)
    rest = (by_walker - high.astype(f32)).astype(bf16)
    g, q = iota((128, 512), 0), iota((128, 512), 1) >> 5
    code = ((q & 2) << 2) | ((q & 12) >> 1) | (q & 1)
    pick = jnp.where(g == (code ^ base), 1.0, 0.0).astype(bf16)
    walkers = jnp.where((iota((512, 128), 0) >> 5) == iota((512, 128), 1), 1.0, 0.0).astype(bf16)
    same = (iota((512, 512), 0) & 31) == (iota((512, 512), 1) & 31)

    def weights(part):
        spread = jnp.dot(part, pick, preferred_element_type=f32).astype(bf16)
        full = jnp.dot(walkers, spread, preferred_element_type=f32)
        return jnp.where(same, full, 0.0).astype(bf16)

    w_high, w_rest = weights(high), weights(rest)
    vectors = jnp.concatenate([held_ref[...], one_ref[...], two_ref[...], three_ref[...]], axis=0)
    for i in range(2):
        rows = slice(256 * i, 256 * i + 256)
        value = jnp.dot(w_rest[rows], vectors, preferred_element_type=f32)
        value += jnp.dot(w_high[rows], vectors, preferred_element_type=f32)
        out_ref[rows, :] = value.astype(bf16)


def taylor_kernel(orb_ref, mine_ref, other_ref, all_hbm, out_ref, op, term_a, term_b, all_ref, sem):
    z, k = lax.axis_index("zl"), lax.axis_index("core")
    gathered = pltpu.make_async_copy(all_hbm, all_ref, sem)
    gathered.start()
    for p in range(16):
        here = pl.multiple_of(64 * p + 32 * k, 32)
        there = pl.multiple_of(64 * p + 32 * (1 - k), 32)
        for d in range(5):
            col = ((p // 2 + d) % 8) * 128
            op[pl.ds(here, 32), col:col + 128] = mine_ref[p, :, 128 * d:128 * d + 128]
            op[pl.ds(there, 32), col:col + 128] = other_ref[p, :, 128 * d:128 * d + 128]
    for i in range(8):
        for d in range(1, 4):
            j = (i + d) % 8
            block = op[128 * i:128 * i + 128, 128 * j:128 * j + 128].astype(f32)
            op[128 * j:128 * j + 128, 128 * i:128 * i + 128] = block.T.astype(bf16)
    gathered.wait()
    term_a[...] = jnp.concatenate([all_ref[...], jnp.zeros((1024, 56), f32)], axis=1).astype(bf16)
    own = pl.multiple_of((2 * z + k) * 64, 64)
    own_rows = op[pl.ds(own, 64), :]
    total = jnp.zeros((64, 256), f32)
    now, later = term_a, term_b
    for degree in range(1, TAYLOR + 1):
        term = now[...]
        total += jnp.dot(own_rows, term, preferred_element_type=f32) * (1.0 / degree)
        if degree < TAYLOR:
            for i in range(4):
                image = jnp.dot(op[256 * i:256 * i + 256, :], term, preferred_element_type=f32)
                later[256 * i:256 * i + 256, :] = (image * (1.0 / degree)).astype(bf16)
            now, later = later, now
    out_ref[...] = orb_ref[...] + total[:, :200]


def call(body, outs, *args, scratch=(), smem=0, hbm=(), grant=40):
    vmem = pl.BlockSpec(memory_space=pltpu.VMEM)
    specs = [pl.BlockSpec(memory_space=pltpu.SMEM)] * smem + [vmem] * (len(args) - smem)
    for i in hbm:
        specs[i] = pl.BlockSpec(memory_space=pl.ANY)
    many = isinstance(outs, (list, tuple))
    return pl.pallas_call(
        body,
        out_shape=outs,
        in_specs=specs,
        out_specs=[vmem] * len(outs) if many else vmem,
        scratch_shapes=list(scratch),
        compiler_params=pltpu.CompilerParams(vmem_limit_bytes=grant * 2**20),
    )(*args)


def shape(dims, dtype):
    return jax.ShapeDtypeStruct(dims, dtype)


def exchange(value, axes):
    return lax.all_to_all(value, axes, 0, 0, tiled=True)


def swap(value, bits):
    return lax.ppermute(value, "zl", [(i, i ^ bits) for i in range(8)])


def shards(orbitals, inverse_intersection, half_rotated, chol_full, fields):
    orb = orbitals[0]
    theta, hr_cut, piece = call(
        first_kernel,
        [shape((14, 8, 128), bf16), shape((16, 8, 128), bf16), shape((32, 640), bf16)],
        fields, orb, inverse_intersection[0], half_rotated[0], chol_full[0],
        scratch=[pltpu.VMEM((64, 200), f32), pltpu.VMEM((200, 200), f32), pltpu.VMEM((200, 1024), bf16),
                 pltpu.VMEM((32, 1024), bf16), pltpu.VMEM((8, 1024), f32), pltpu.VMEM((8, 1024), f32),
                 pltpu.SemaphoreType.DMA((4,))],
        smem=1, hbm=(1, 2, 3, 4), grant=60,
    )
    everyone = lax.all_gather(orb, CHOL, axis=0, tiled=True)
    pairs = [(k * 2 + h, h * 2 + k) for k in range(2) for h in range(2)]
    cross = [(k * 2 + h, h * 2 + 1 - k) for k in range(2) for h in range(2)]
    straight = lax.ppermute(piece, ("core", "zh"), pairs)
    crossed = lax.ppermute(piece, ("core", "zh"), cross)
    hr_all = exchange(hr_cut, CHOL)
    straight, crossed, hr_all = lax.optimization_barrier((straight, crossed, hr_all))
    held = jnp.concatenate([straight, crossed], axis=0)
    four = swap(held, 4)
    spread = call(spread_kernel, shape((16, 30, 8, 128), bf16), hr_all, theta)
    in_plane = exchange(spread, PLANE)
    four, in_plane = lax.optimization_barrier((four, in_plane))
    held = jnp.concatenate([held, four], axis=0)
    one, two, three = swap(held, 1), swap(held, 2), swap(held, 3)
    partial = call(bias_kernel, shape((16, 16, 128), f32), in_plane)
    everywhere = exchange(partial, CHOL)
    pieces = call(operator_kernel, shape((512, 640), bf16), everywhere, held, one, two, three)
    mine = exchange(pieces.reshape(16, 32, 640), PLANE)
    other = lax.ppermute(mine, "core", [(0, 1), (1, 0)])
    out = call(
        taylor_kernel, shape((64, 200), f32), orb, mine, other, everyone,
        scratch=[pltpu.VMEM((1024, 1024), bf16), pltpu.VMEM((1024, 256), bf16), pltpu.VMEM((1024, 256), bf16),
                 pltpu.VMEM((1024, 200), f32), pltpu.SemaphoreType.DMA(())],
        hbm=(3,), grant=60,
    )
    return out[None]


def solution(mesh):
    fine = Mesh(mesh.devices.reshape(8, 2, 4, 4, 2), ("zl", "core", "y", "x", "zh"))
    return jax.shard_map(
        shards,
        mesh=fine,
        in_specs=(
            P(WALK, CHOL, None),
            P(WALK, None, None),
            P(CHOL, None, None),
            P(CHOL, WALK, None),
            P(CHOL, WALK),
        ),
        out_specs=P(WALK, CHOL, None),
        check_vma=False,
    )
```

time: 123 us -> 157 us (1.28)
  blocking collectives: 37.1 us -> 56.3 us
  starting transfers between devices: 48 us -> 62.1 us
  Pallas kernels: 8.11 us -> 13.1 us
  local copies, waits for them, and re-layouts: 3.64 us -> 0.88 us
    all_gather x0 -> x1, blocking collectives: none -> 38.5 us  [shards(): everyone = lax.all_gather(orb, CHOL, axis=0, tiled=True)]
    all_to_all x3 -> x1, blocking collectives: 37.1 us -> 17.8 us  [exchange(): return lax.all_to_all(value, axes, 0, 0, tiled=True)]
    all_to_all x2 -> x3, starting transfers between devices: 11.8 us -> 30.2 us  [exchange(): return lax.all_to_all(value, axes, 0, 0, tiled=True)]
    all_to_all x2 -> x3, waiting for transfers between devices: 14 us -> 1.93 us  [exchange(): return lax.all_to_all(value, axes, 0, 0, tiled=True)]
    ppermute x5, waiting for transfers between devices: 5.02 us -> 15.1 us  [the longest x4 15.1 us: swap(): return lax.ppermute(value, 'zl', [(i, i ^ bits) for i in range(8)])]
    ppermute x1, starting transfers between devices: 8.77 us -> 2.01 us  [shards(): crossed = lax.ppermute(piece, ('core', 'zh'), cross)]
    pallas_call x5, Pallas kernels: 8.11 us -> 13.1 us  [call(): pl.pallas_call(body, out_shape=outs, in_specs=specs, out_specs=[vmem] * l...]
    ppermute x5, starting transfers between devices: 17.5 us -> 21.6 us  [the longest x4 17.3 us: swap(): return lax.ppermute(value, 'zl', [(i, i ^ bits) for i in range(8)])]
  transfers between devices with their start and end apart: 9 -> 10, of which waited for: 5 -> 6; matrix products, arithmetic and copies ran while one was open for 0% -> 0% of each run, Pallas kernels for 1% -> 0%
where the time goes in v2:
time: 157 us; the launch traced here: 156 us
  starting transfers between devices  62.1 us (40%)
  blocking collectives  56.3 us (36%)
  waiting for transfers between devices  22.9 us (15%)
  Pallas kernels  13.1 us (8%)
    all_gather x1, blocking collectives, shards(): everyone = lax.all_gather(orb, CHOL, axis=0, tiled=True)  38.5 us
    all_to_all x3, starting transfers between devices, exchange(): return lax.all_to_all(value, axes, 0, 0, tiled=True)  30.2 us
    all_to_all x1, blocking collectives, exchange(): return lax.all_to_all(value, axes, 0, 0, tiled=True)  17.8 us
    ppermute x4, starting transfers between devices, swap(): return lax.ppermute(value, 'zl', [(i, i ^ bits) for i in range(8)])  17.3 us
    ppermute x4, waiting for transfers between devices, swap(): return lax.ppermute(value, 'zl', [(i, i ^ bits) for i in range(8)])  15.1 us
    pallas_call x5, Pallas kernels, call(): pl.pallas_call(body, out_shape=outs, in_specs=specs, out_specs=[vmem] * l...  13.1 us
    ppermute x1, starting transfers between devices, shards(): straight = lax.ppermute(piece, ('core', 'zh'), pairs)  8.23 us
    ppermute x1, starting transfers between devices, shards(): other = lax.ppermute(mine, 'core', [(0, 1), (1, 0)])  4.3 us
  transfers between devices with their start and end apart: 10, of which 6 were waited for; matrix products, arithmetic and copies ran while one was open for 0% of the time, Pallas kernels for 0%

profile of v2, /device:TPU:1, one launch (start us, length us, event | category | flops | bytes accessed | tf_op | source)
XLA Modules:
  0.0 156.0 jit_solution(497751617402804133)
XLA Ops:
  0.7 2.2 %shard_map.55 = (bf16[14,8,128]{2,1,0:T(8,128)(2,1)}, bf16[16,8,128]{2,1,0:T(8,128)(2,1)}, bf16[32,640]{1,0:T(8,128)(2,1)}) custom-call(f32[1,1]{1,0:T(1,128)S(6)} %copy.8.field_ref, f32[64,200]{1,0:T(8,128)} %bitcast.9, f32[200,200]{1,0:T(8,128)} %bitcast.12, bf16[200,1024]{1,0:T(8,128)(2,1)} %bitcast.11, bf16[32,1024]{1,0:T(8,128)(2,1)} %bitcast.13), custom_call_target="tpu_custom_call" | custom-call | tf_op jit(solution)/shard_map/pallas_call | solution.py:174
  2.8 14.2 %all-to-all-start = ((bf16[16,8,128]{2,1,0:T(8,128)(2,1)}), bf16[16,8,128]{2,1,0:T(8,128)(2,1)S(1)}, u32[]{:S(2)}, u32[]{:S(2)}) async-start(bf16[16,8,128]{2,1,0:T(8,128)(2,1)} %get-tuple-element.14), calls=%async_computation | async-start | bytes 65536 | tf_op jit(solution)/shard_map/all_to_all | solution.py:189
  17.0 2.0 %collective-permute-start.1 = (bf16[32,640]{1,0:T(8,128)(2,1)S(1)}, bf16[32,640]{1,0:T(8,128)(2,1)S(1)}, u32[]{:S(2)}, u32[]{:S(2)}) collective-permute-start(bf16[32,640]{1,0:T(8,128)(2,1)S(1)} %copy-done.4), channel_id=1, source_target_pairs={{0,1},{1,33},{32,0},{33,32},{2,3},{3,35},{34,2},{35,34},{4,5},{5,3... | collective-permute-start | bytes 122888 | tf_op jit(solution)/shard_map/ppermute | solution.py:211
  19.1 8.2 %collective-permute-start = (bf16[32,640]{1,0:T(8,128)(2,1)S(1)}, bf16[32,640]{1,0:T(8,128)(2,1)S(1)}, u32[]{:S(2)}, u32[]{:S(2)}) collective-permute-start(bf16[32,640]{1,0:T(8,128)(2,1)S(1)} %copy-done.4), channel_id=1, source_target_pairs={{0,0},{1,32},{32,1},{33,33},{2,2},{3,34},{34,3},{35,35},{4,4},{5,3... | collective-permute-start | bytes 122888 | tf_op jit(solution)/shard_map/ppermute | solution.py:210
  27.3 3.3 %collective-permute-done.1 = bf16[32,640]{1,0:T(8,128)(2,1)S(1)} collective-permute-done((bf16[32,640]{1,0:T(8,128)(2,1)S(1)}, bf16[32,640]{1,0:T(8,128)(2,1)S(1)}, u32[]{:S(2)}, u32[]{:S(2)}) %collective-permute-start.1) | collective-permute-done | bytes 40992 | tf_op jit(solution)/shard_map/ppermute | solution.py:211
  30.6 2.5 %collective-permute-done = bf16[32,640]{1,0:T(8,128)(2,1)S(1)} collective-permute-done((bf16[32,640]{1,0:T(8,128)(2,1)S(1)}, bf16[32,640]{1,0:T(8,128)(2,1)S(1)}, u32[]{:S(2)}, u32[]{:S(2)}) %collective-permute-start) | collective-permute-done | bytes 40992 | tf_op jit(solution)/shard_map/ppermute | solution.py:210
  33.1 1.1 shard_map.56
  34.2 6.8 %all-to-all-start.1 = ((bf16[16,30,8,128]{3,2,1,0:T(8,128)(2,1)}), bf16[16,30,8,128]{3,2,1,0:T(8,128)(2,1)S(1)}, u32[]{:S(2)}, u32[]{:S(2)}) async-start(bf16[16,30,8,128]{3,2,1,0:T(8,128)(2,1)} %shard_map.56), calls=%async_computation.1 | async-start | bytes 1966080 | tf_op jit(solution)/shard_map/all_to_all | solution.py:189
  41.0 8.0 %collective-permute-start.2 = (bf16[64,640]{1,0:T(8,128)(2,1)S(1)}, bf16[64,640]{1,0:T(8,128)(2,1)S(1)}, u32[]{:S(2)}, u32[]{:S(2)}) collective-permute-start(bf16[64,640]{1,0:T(8,128)(2,1)S(1)} %pad_maximum_fusion), channel_id=1, source_target_pairs={{0,256},{64,320},{128,384},{192,448},{256,0},{320,64},{384,128},{4... | collective-permute-start | bytes 245768 | tf_op jit(solution)/shard_map/ppermute | solution.py:193
  49.0 2.7 %collective-permute-done.2 = bf16[64,640]{1,0:T(8,128)(2,1)S(1)} collective-permute-done((bf16[64,640]{1,0:T(8,128)(2,1)S(1)}, bf16[64,640]{1,0:T(8,128)(2,1)S(1)}, u32[]{:S(2)}, u32[]{:S(2)}) %collective-permute-start.2) | collective-permute-done | bytes 81952 | tf_op jit(solution)/shard_map/ppermute | solution.py:193
  51.7 1.9 %all-to-all-done.1.in_ref = bf16[16,30,8,128]{3,2,1,0:T(8,128)(2,1)S(1)} async-done(((bf16[16,30,8,128]{3,2,1,0:T(8,128)(2,1)}), bf16[16,30,8,128]{3,2,1,0:T(8,128)(2,1)S(1)}, u32[]{:S(2)}, u32[]{:S(2)}) %all-to-all-start.1) | async-done | bytes 983072 | tf_op jit(solution)/shard_map/all_to_all | solution.py:189
  53.6 1.3 shard_map.57
  54.9 9.3 %all-to-all-start.2 = ((f32[16,16,128]{2,1,0:T(8,128)}), f32[16,16,128]{2,1,0:T(8,128)S(1)}, u32[]{:S(2)}, u32[]{:S(2)}) async-start(f32[16,16,128]{2,1,0:T(8,128)} %shard_map.57), calls=%async_computation.2 | async-start | bytes 262144 | tf_op jit(solution)/shard_map/all_to_all | solution.py:189
  64.3 5.1 %collective-permute-start.5 = (bf16[128,640]{1,0:T(8,128)(2,1)S(1)}, bf16[128,640]{1,0:T(8,128)(2,1)S(1)}, u32[]{:S(2)}, u32[]{:S(2)}) collective-permute-start(bf16[128,640]{1,0:T(8,128)(2,1)S(1)} %constant_dynamic-update-slice_fusion.held_ref), channel_id=1, source_target_pairs={{0,192},{64,128},{128,64},{192,0},{256,448},{320,384},{384,320},{4... | collective-permute-start | bytes 491528 | tf_op jit(solution)/shard_map/ppermute | solution.py:193
  69.4 1.9 %collective-permute-start.4 = (bf16[128,640]{1,0:T(8,128)(2,1)S(1)}, bf16[128,640]{1,0:T(8,128)(2,1)S(1)}, u32[]{:S(2)}, u32[]{:S(2)}) collective-permute-start(bf16[128,640]{1,0:T(8,128)(2,1)S(1)} %constant_dynamic-update-slice_fusion.held_ref), channel_id=1, source_target_pairs={{0,128},{64,192},{128,0},{192,64},{256,384},{320,448},{384,256},{4... | collective-permute-start | bytes 491528 | tf_op jit(solution)/shard_map/ppermute | solution.py:193
  71.3 2.3 %collective-permute-start.3 = (bf16[128,640]{1,0:T(8,128)(2,1)S(1)}, bf16[128,640]{1,0:T(8,128)(2,1)S(1)}, u32[]{:S(2)}, u32[]{:S(2)}) collective-permute-start(bf16[128,640]{1,0:T(8,128)(2,1)S(1)} %constant_dynamic-update-slice_fusion.held_ref), channel_id=1, source_target_pairs={{0,64},{64,0},{128,192},{192,128},{256,320},{320,256},{384,448},{4... | collective-permute-start | bytes 491528 | tf_op jit(solution)/shard_map/ppermute | solution.py:193
  73.6 4.0 %collective-permute-done.5.three_ref = bf16[128,640]{1,0:T(8,128)(2,1)S(1)} collective-permute-done((bf16[128,640]{1,0:T(8,128)(2,1)S(1)}, bf16[128,640]{1,0:T(8,128)(2,1)S(1)}, u32[]{:S(2)}, u32[]{:S(2)}) %collective-permute-start.5) | collective-permute-done | bytes 163872 | tf_op jit(solution)/shard_map/ppermute | solution.py:193
  77.6 8.4 %collective-permute-done.4.two_ref = bf16[128,640]{1,0:T(8,128)(2,1)S(1)} collective-permute-done((bf16[128,640]{1,0:T(8,128)(2,1)S(1)}, bf16[128,640]{1,0:T(8,128)(2,1)S(1)}, u32[]{:S(2)}, u32[]{:S(2)}) %collective-permute-start.4) | collective-permute-done | bytes 163872 | tf_op jit(solution)/shard_map/ppermute | solution.py:193
  86.1 1.7 %shard_map.58 = bf16[512,640]{1,0:T(8,128)(2,1)S(1)} custom-call(f32[16,16,128]{2,1,0:T(8,128)S(1)} %all-to-all-done.2.in_ref, bf16[128,640]{1,0:T(8,128)(2,1)S(1)} %constant_dynamic-update-slice_fusion.held_ref, bf16[128,640]{1,0:T(8,128)(2,1)S(1)} %collective-permute-done.3.one_ref, bf16[128,640]{1,0:T(8,128)(2,1)S(1)} %collective-permute-done.4.two_ref, ...), custom_call_target="tpu_custom_call" | custom-call | tf_op jit(solution)/shard_map/pallas_call | solution.py:174
  87.8 17.8 %all_to_all.20.mine_ref = bf16[16,32,640]{2,1,0:T(8,128)(2,1)S(1)} all-to-all(bf16[16,32,640]{2,1,0:T(8,128)(2,1)S(1)} %bitcast.7), channel_id=1, replica_groups=mesh['zl'=8,'core'=2,'y'=4,'x'=4,'zh'=2] {'y','x'}, dimensions={0} | all-to-all | bytes 1310720 | tf_op jit(solution)/shard_map/all_to_all | solution.py:189
  105.6 4.3 %collective-permute-start.6 = (bf16[16,32,640]{2,1,0:T(8,128)(2,1)S(1)}, bf16[16,32,640]{2,1,0:T(8,128)(2,1)S(1)}, u32[]{:S(2)}, u32[]{:S(2)}) collective-permute-start(bf16[16,32,640]{2,1,0:T(8,128)(2,1)S(1)} %all_to_all.20.mine_ref), channel_id=1, source_target_pairs={{0,32},{32,0},{1,33},{33,1},{2,34},{34,2},{3,35},{35,3},{4,36},{36... | collective-permute-start | bytes 1966088 | tf_op jit(solution)/shard_map/ppermute | solution.py:225
  109.9 38.5 %all-gather = f32[1,1024,200]{2,1,0:T(8,128)} all-gather(f32[1,64,200]{2,1,0:T(8,128)S(1)} %copy-done.3), channel_id=2, replica_groups=mesh['zl'=8,'core'=2,'y'=4,'x'=4,'zh'=2] {'zl','core'}, dimensions={1}, use_global_device_ids=true | all-gather | bytes 870400 | tf_op jit(solution)/shard_map/all_gather | solution.py:207
  148.4 0.8 copy-done.2
  149.3 6.8 %shard_map.59 = f32[64,200]{1,0:T(8,128)} custom-call(f32[64,200]{1,0:T(8,128)} %bitcast.10, bf16[16,32,640]{2,1,0:T(8,128)(2,1)} %copy-done.1, bf16[16,32,640]{2,1,0:T(8,128)(2,1)} %copy-done.2, f32[1024,200]{1,0:T(8,128)} %bitcast.8), custom_call_target="tpu_custom_call" | custom-call | tf_op jit(solution)/shard_map/pallas_call | solution.py:174
  (17 shorter events, 0.1 us)
Async XLA Ops:
  2.8 14.2 %copy-start.4 = (bf16[32,640]{1,0:T(8,128)(2,1)S(1)}, bf16[32,640]{1,0:T(8,128)(2,1)}, u32[]{:S(2)}) copy-start(bf16[32,640]{1,0:T(8,128)(2,1)} %get-tuple-element.13) | copy-start | bytes 122884
  2.8 30.3 %copy-start = (bf16[14,8,128]{2,1,0:T(8,128)(2,1)S(1)}, bf16[14,8,128]{2,1,0:T(8,128)(2,1)}, u32[]{:S(2)}) copy-start(bf16[14,8,128]{2,1,0:T(8,128)(2,1)} %get-tuple-element.18.theta_ref) | copy-start | bytes 86020
  2.8 30.3 %all-to-all-start = ((bf16[16,8,128]{2,1,0:T(8,128)(2,1)}), bf16[16,8,128]{2,1,0:T(8,128)(2,1)S(1)}, u32[]{:S(2)}, u32[]{:S(2)}) async-start(bf16[16,8,128]{2,1,0:T(8,128)(2,1)} %get-tuple-element.14), calls=%async_computation | async-start | bytes 65536 | tf_op jit(solution)/shard_map/all_to_all | solution.py:189
  17.0 13.5 %collective-permute-start.1 = (bf16[32,640]{1,0:T(8,128)(2,1)S(1)}, bf16[32,640]{1,0:T(8,128)(2,1)S(1)}, u32[]{:S(2)}, u32[]{:S(2)}) collective-permute-start(bf16[32,640]{1,0:T(8,128)(2,1)S(1)} %copy-done.4), channel_id=1, source_target_pairs={{0,1},{1,33},{32,0},{33,32},{2,3},{3,35},{34,2},{35,34},{4,5},{5,3... | collective-permute-start | bytes 122888 | tf_op jit(solution)/shard_map/ppermute | solution.py:211
  19.1 14.0 %collective-permute-start = (bf16[32,640]{1,0:T(8,128)(2,1)S(1)}, bf16[32,640]{1,0:T(8,128)(2,1)S(1)}, u32[]{:S(2)}, u32[]{:S(2)}) collective-permute-start(bf16[32,640]{1,0:T(8,128)(2,1)S(1)} %copy-done.4), channel_id=1, source_target_pairs={{0,0},{1,32},{32,1},{33,33},{2,2},{3,34},{34,3},{35,35},{4,4},{5,3... | collective-permute-start | bytes 122888 | tf_op jit(solution)/shard_map/ppermute | solution.py:210
  34.2 19.4 %all-to-all-start.1 = ((bf16[16,30,8,128]{3,2,1,0:T(8,128)(2,1)}), bf16[16,30,8,128]{3,2,1,0:T(8,128)(2,1)S(1)}, u32[]{:S(2)}, u32[]{:S(2)}) async-start(bf16[16,30,8,128]{3,2,1,0:T(8,128)(2,1)} %shard_map.56), calls=%async_computation.1 | async-start | bytes 1966080 | tf_op jit(solution)/shard_map/all_to_all | solution.py:189
  41.0 10.7 %collective-permute-start.2 = (bf16[64,640]{1,0:T(8,128)(2,1)S(1)}, bf16[64,640]{1,0:T(8,128)(2,1)S(1)}, u32[]{:S(2)}, u32[]{:S(2)}) collective-permute-start(bf16[64,640]{1,0:T(8,128)(2,1)S(1)} %pad_maximum_fusion), channel_id=1, source_target_pairs={{0,256},{64,320},{128,384},{192,448},{256,0},{320,64},{384,128},{4... | collective-permute-start | bytes 245768 | tf_op jit(solution)/shard_map/ppermute | solution.py:193
  54.9 31.1 %all-to-all-start.2 = ((f32[16,16,128]{2,1,0:T(8,128)}), f32[16,16,128]{2,1,0:T(8,128)S(1)}, u32[]{:S(2)}, u32[]{:S(2)}) async-start(f32[16,16,128]{2,1,0:T(8,128)} %shard_map.57), calls=%async_computation.2 | async-start | bytes 262144 | tf_op jit(solution)/shard_map/all_to_all | solution.py:189
  64.3 13.3 %collective-permute-start.5 = (bf16[128,640]{1,0:T(8,128)(2,1)S(1)}, bf16[128,640]{1,0:T(8,128)(2,1)S(1)}, u32[]{:S(2)}, u32[]{:S(2)}) collective-permute-start(bf16[128,640]{1,0:T(8,128)(2,1)S(1)} %constant_dynamic-update-slice_fusion.held_ref), channel_id=1, source_target_pairs={{0,192},{64,128},{128,64},{192,0},{256,448},{320,384},{384,320},{4... | collective-permute-start | bytes 491528 | tf_op jit(solution)/shard_map/ppermute | solution.py:193
  69.4 16.7 %collective-permute-start.4 = (bf16[128,640]{1,0:T(8,128)(2,1)S(1)}, bf16[128,640]{1,0:T(8,128)(2,1)S(1)}, u32[]{:S(2)}, u32[]{:S(2)}) collective-permute-start(bf16[128,640]{1,0:T(8,128)(2,1)S(1)} %constant_dynamic-update-slice_fusion.held_ref), channel_id=1, source_target_pairs={{0,128},{64,192},{128,0},{192,64},{256,384},{320,448},{384,256},{4... | collective-permute-start | bytes 491528 | tf_op jit(solution)/shard_map/ppermute | solution.py:193
  71.3 14.7 %collective-permute-start.3 = (bf16[128,640]{1,0:T(8,128)(2,1)S(1)}, bf16[128,640]{1,0:T(8,128)(2,1)S(1)}, u32[]{:S(2)}, u32[]{:S(2)}) collective-permute-start(bf16[128,640]{1,0:T(8,128)(2,1)S(1)} %constant_dynamic-update-slice_fusion.held_ref), channel_id=1, source_target_pairs={{0,64},{64,0},{128,192},{192,128},{256,320},{320,256},{384,448},{4... | collective-permute-start | bytes 491528 | tf_op jit(solution)/shard_map/ppermute | solution.py:193
  87.8 22.1 %copy-start.3 = (f32[1,64,200]{2,1,0:T(8,128)S(1)}, f32[1,64,200]{2,1,0:T(8,128)}, u32[]{:S(2)}) copy-start(f32[1,64,200]{2,1,0:T(8,128)} %param.5) | copy-start | bytes 153604
  105.6 42.8 %copy-start.1 = (bf16[16,32,640]{2,1,0:T(8,128)(2,1)}, bf16[16,32,640]{2,1,0:T(8,128)(2,1)S(1)}, u32[]{:S(2)}) copy-start(bf16[16,32,640]{2,1,0:T(8,128)(2,1)S(1)} %all_to_all.20.mine_ref) | copy-start | bytes 1966084
  105.6 42.8 %collective-permute-start.6 = (bf16[16,32,640]{2,1,0:T(8,128)(2,1)S(1)}, bf16[16,32,640]{2,1,0:T(8,128)(2,1)S(1)}, u32[]{:S(2)}, u32[]{:S(2)}) collective-permute-start(bf16[16,32,640]{2,1,0:T(8,128)(2,1)S(1)} %all_to_all.20.mine_ref), channel_id=1, source_target_pairs={{0,32},{32,0},{1,33},{33,1},{2,34},{34,2},{3,35},{35,3},{4,36},{36... | collective-permute-start | bytes 1966088 | tf_op jit(solution)/shard_map/ppermute | solution.py:225
  148.4 0.8 copy-start.2

commit v3 on v1

v3 whole, which is shorter than its diff:
```python
import jax
import jax.numpy as jnp
from jax import lax
from jax.experimental import pallas as pl
from jax.experimental.pallas import tpu as pltpu
from jax.sharding import Mesh, PartitionSpec as P

TAYLOR = 5
field_scale = 0.4
f32, bf16 = jnp.float32, jnp.bfloat16

CHOL = ("zl", "core")
WALK = ("y", "x", "zh")
PLANE = ("y", "x")
RING = ("zh", "zl")


def iota(shape, dim):
    return lax.broadcasted_iota(jnp.int32, shape, dim)


def plane_index():
    return lax.axis_index("y") * 4 + lax.axis_index("x")


def chol_index():
    return lax.axis_index("zl") * 2 + lax.axis_index("core")


def pack_kernel(orb_hbm, chol_hbm, out_ref, orb_ref, chol_ref, sems):
    copies = [pltpu.make_async_copy(chol_hbm, chol_ref, sems.at[0]), pltpu.make_async_copy(orb_hbm, orb_ref, sems.at[1])]
    for copy in copies:
        copy.start()
    p = plane_index()
    start = p // 2

    def block(d):
        col = pl.multiple_of(lax.rem(start + d, 8) * 128, 128)
        return chol_ref[:, pl.ds(col, 128)]

    copies[0].wait()
    for d in range(4):
        out_ref[:, 128 * d:128 * d + 128] = block(d)
    last = block(4).astype(f32)
    half = jnp.bitwise_xor(jnp.bitwise_and(p, 1), (start >= 4).astype(jnp.int32))
    last = jnp.where(half == 1, pltpu.roll(last, 64, 1), last)
    copies[1].wait()
    low = jnp.concatenate([orb_ref[...], jnp.zeros((64, 56), f32)], axis=1)
    top, bottom = low[0:32], low[32:64]
    lane = iota((32, 128), 1)
    out_ref[:, 512:640] = jnp.where(lane < 64, last, pltpu.roll(bottom[:, 128:256], 64, 1)).astype(bf16)
    out_ref[:, 640:768] = top[:, 0:128].astype(bf16)
    out_ref[:, 768:896] = bottom[:, 0:128].astype(bf16)
    ends = jnp.where(lane < 72, top[:, 128:256], pltpu.roll(bottom[:, 128:256], 8, 1))
    out_ref[:, 896:976] = ends[:, 0:80].astype(bf16)


def select_kernel(ring_ref, own_ref, send_ref):
    k, h = lax.axis_index("core"), lax.axis_index("zh")
    lane = iota((32, 128), 1)
    for j in range(8):
        for half, target in ((k, own_ref), (1 - k, send_ref)):
            target[j, :, 0:512] = ring_ref[half, j, :, 0:512]
            tail = ring_ref[half, j, :, 512:640].astype(f32)
            target[j, :, 512:640] = jnp.where(lane < 64, tail, 0.0).astype(bf16)
        middle = ring_ref[h, j, :, 512:640].astype(f32)
        ends = jnp.concatenate([ring_ref[h, j, :, 896:976].astype(f32), jnp.zeros((32, 48), f32)], axis=1)
        top = jnp.where(lane < 72, ends, 0.0).astype(bf16)
        bottom = jnp.where(lane < 64, pltpu.roll(middle, 64, 1), jnp.where(lane < 72, pltpu.roll(ends, 120, 1), 0.0))
        bottom = bottom.astype(bf16)
        for target in (own_ref, send_ref):
            target[j, :, 640:768] = ring_ref[h, j, :, 640:768]
            target[j, :, 768:896] = top
            target[j, :, 896:1024] = ring_ref[h, j, :, 768:896]
            target[j, :, 1024:1152] = bottom


def bias_kernel(field_ref, own_ref, got_ref, inv_ref, hr_ref, term_ref, out_ref, inv_low, inv_high):
    k = lax.axis_index("core")
    for j in range(8):
        for source, core in ((own_ref, k), (got_ref, 1 - k)):
            row = pl.multiple_of((2 * j + core) * 64, 64)
            term_ref[pl.ds(row, 32), :] = source[j, :, 640:896]
            term_ref[pl.ds(row + 32, 32), :] = source[j, :, 896:1152]
    inverse = inv_ref[...]
    wide = jnp.concatenate([inverse, jnp.zeros((200, 56), f32)], axis=1)
    full = jnp.concatenate([wide, jnp.zeros((56, 256), f32)], axis=0)
    high = full.astype(bf16)
    inv_high[...] = high
    inv_low[...] = (full - high.astype(f32)).astype(bf16)
    term = term_ref[...]
    theta = jnp.dot(term, inv_high[...], preferred_element_type=f32)
    theta += jnp.dot(term, inv_low[...], preferred_element_type=f32)
    theta_high = theta.astype(bf16)
    theta_low = (theta - theta_high.astype(f32)).astype(bf16)
    rotated = hr_ref[...]
    product = jnp.dot(rotated, theta_high, preferred_element_type=f32)
    product += jnp.dot(rotated, theta_low, preferred_element_type=f32)
    diagonal = jnp.where(iota((200, 256), 0) == iota((200, 256), 1), product, 0.0)
    raw_bias = jnp.sum(jnp.sum(diagonal, axis=0, keepdims=True), axis=1, keepdims=True)
    shifted = field_scale * (field_ref[0, 0] - jnp.clip(raw_bias, -1.0, 1.0))
    here = (iota((16, 128), 0) == chol_index()) & (iota((16, 128), 1) == plane_index())
    tile = jnp.where(here, shifted, 0.0)
    for j in range(16):
        out_ref[j] = tile


def sum_kernel(in_ref, out_ref):
    tile = jnp.sum(in_ref[...], axis=0)
    for j in range(16):
        out_ref[j] = tile


def operator_kernel(in_ref, own_ref, got_ref, out_ref):
    k = lax.axis_index("core")
    shifted = jnp.sum(in_ref[...], axis=0)
    by_walker = jnp.concatenate([shifted, jnp.zeros((112, 128), f32)], axis=0).T
    high = by_walker.astype(bf16)
    rest = (by_walker - high.astype(f32)).astype(bf16)
    g, q = iota((128, 512), 0), iota((128, 512), 1) >> 5
    vector = 2 * (q & 7) + jnp.where(q < 8, k, 1 - k)
    pick = jnp.where(g == vector, 1.0, 0.0).astype(bf16)
    walkers = jnp.where((iota((512, 128), 0) >> 5) == iota((512, 128), 1), 1.0, 0.0).astype(bf16)
    same = (iota((512, 512), 0) & 31) == (iota((512, 512), 1) & 31)

    def weights(part):
        spread = jnp.dot(part, pick, preferred_element_type=f32).astype(bf16)
        full = jnp.dot(walkers, spread, preferred_element_type=f32)
        return jnp.where(same, full, 0.0).astype(bf16)

    w_high, w_rest = weights(high), weights(rest)
    own = own_ref[:, :, 0:640].reshape(256, 640)
    got = got_ref[:, :, 0:640].reshape(256, 640)
    vectors = jnp.concatenate([own, got], axis=0)
    for i in range(2):
        rows = slice(256 * i, 256 * i + 256)
        value = jnp.dot(w_rest[rows], vectors, preferred_element_type=f32)
        value += jnp.dot(w_high[rows], vectors, preferred_element_type=f32)
        out_ref[rows, :] = value.astype(bf16)


def taylor_kernel(orb_ref, mine_ref, other_ref, first_ref, out_ref, op, tail, term_a, term_b):
    k = lax.axis_index("core")
    for p in range(16):
        here = pl.multiple_of(64 * p + 32 * k, 32)
        there = pl.multiple_of(64 * p + 32 * (1 - k), 32)
        for row, source in ((here, mine_ref), (there, other_ref)):
            for d in range(4):
                col = ((p // 2 + d) % 8) * 128
                op[pl.ds(row, 32), col:col + 128] = source[p, :, 128 * d:128 * d + 128]
            tail[pl.ds(row, 32), :] = source[p, :, 512:640].astype(f32)
    for i in range(8):
        for d in range(1, 4):
            j = (i + d) % 8
            block = op[128 * i:128 * i + 128, 128 * j:128 * j + 128].astype(f32)
            op[128 * j:128 * j + 128, 128 * i:128 * i + 128] = block.T.astype(bf16)
    left = iota((64, 128), 1) < 64
    for i in range(4):
        j = i + 4
        near = tail[128 * i:128 * i + 128, :]
        far = tail[128 * j:128 * j + 128, :].T[0:64]
        top = jnp.where(left, near[0:64], far)
        bottom = jnp.where(left, far, pltpu.roll(near[64:128], 64, 1))
        block = jnp.concatenate([top, bottom], axis=0)
        op[128 * i:128 * i + 128, 128 * j:128 * j + 128] = block.astype(bf16)
        op[128 * j:128 * j + 128, 128 * i:128 * i + 128] = block.T.astype(bf16)
    own = pl.multiple_of(chol_index() * 64, 64)
    own_rows = op[pl.ds(own, 64), :]
    total = jnp.zeros((64, 256), f32)
    now, later, spare = first_ref, term_a, term_b
    for degree in range(1, TAYLOR + 1):
        term = now[...]
        total += jnp.dot(own_rows, term, preferred_element_type=f32) * (1.0 / degree)
        if degree < TAYLOR:
            for i in range(4):
                image = jnp.dot(op[256 * i:256 * i + 256, :], term, preferred_element_type=f32)
                later[256 * i:256 * i + 256, :] = (image * (1.0 / degree)).astype(bf16)
            now, later, spare = later, spare, later
    out_ref[...] = orb_ref[...] + total[:, :200]


def call(body, outs, *args, scratch=(), smem=0, hbm=(), grant=40):
    vmem = pl.BlockSpec(memory_space=pltpu.VMEM)
    specs = [pl.BlockSpec(memory_space=pltpu.SMEM)] * smem + [vmem] * (len(args) - smem)
    for i in hbm:
        specs[i] = pl.BlockSpec(memory_space=pl.ANY)
    many = isinstance(outs, (list, tuple))
    return pl.pallas_call(
        body,
        out_shape=outs,
        in_specs=specs,
        out_specs=[vmem] * len(outs) if many else vmem,
        scratch_shapes=list(scratch),
        compiler_params=pltpu.CompilerParams(vmem_limit_bytes=grant * 2**20),
    )(*args)


def shape(dims, dtype):
    return jax.ShapeDtypeStruct(dims, dtype)


def exchange(value, axes):
    return lax.all_to_all(value, axes, 0, 0, tiled=True)


def shards(orbitals, inverse_intersection, half_rotated, chol_full, fields):
    orb = orbitals[0]
    packed = call(
        pack_kernel, shape((32, 976), bf16), orb, chol_full[0],
        scratch=[pltpu.VMEM((64, 200), f32), pltpu.VMEM((32, 1024), bf16), pltpu.SemaphoreType.DMA((2,))],
        hbm=(0, 1), grant=60,
    )
    ring = lax.all_gather(packed, RING, axis=0, tiled=True)
    own, send = call(select_kernel, [shape((8, 32, 1152), bf16)] * 2, ring.reshape(2, 8, 32, 976))
    swap_core = [(0, 1), (1, 0)]
    got = lax.ppermute(send, "core", swap_core)
    first, partial = call(
        bias_kernel, [shape((1024, 256), bf16), shape((16, 16, 128), f32)],
        fields, own, got, inverse_intersection[0], half_rotated[0],
        scratch=[pltpu.VMEM((256, 256), bf16), pltpu.VMEM((256, 256), bf16)], smem=1,
    )
    in_plane = exchange(partial, PLANE)
    summed = call(sum_kernel, shape((16, 16, 128), f32), in_plane)
    everywhere = exchange(summed, CHOL)
    pieces = call(operator_kernel, shape((512, 640), bf16), everywhere, own, got)
    mine = exchange(pieces.reshape(16, 32, 640), PLANE)
    other = lax.ppermute(mine, "core", swap_core)
    out = call(
        taylor_kernel, shape((64, 200), f32), orb, mine, other, first,
        scratch=[pltpu.VMEM((1024, 1024), bf16), pltpu.VMEM((1024, 128), f32),
                 pltpu.VMEM((1024, 256), bf16), pltpu.VMEM((1024, 256), bf16)],
    )
    return out[None]


def solution(mesh):
    fine = Mesh(mesh.devices.reshape(8, 2, 4, 4, 2), ("zl", "core", "y", "x", "zh"))
    return jax.shard_map(
        shards,
        mesh=fine,
        in_specs=(
            P(WALK, CHOL, None),
            P(WALK, None, None),
            P(CHOL, None, None),
            P(CHOL, WALK, None),
            P(CHOL, WALK),
        ),
        out_specs=P(WALK, CHOL, None),
        check_vma=False,
    )
```

time: 123 us -> 109 us (0.89); the launches traced: 121 us -> 108 us
  blocking collectives: 37.1 us -> 83.5 us
  starting transfers between devices: 48 us -> 12.5 us
  waiting for transfers between devices: 23 us -> 2.66 us
  local copies, waits for them, and re-layouts: 3.64 us -> 0.01 us
    all_gather x0 -> x1, blocking collectives: none -> 36.1 us  [shards(): ring = lax.all_gather(packed, RING, axis=0, tiled=True)]
    ppermute x6 -> x1, starting transfers between devices: 32.1 us -> 9.24 us  [shards(): got = lax.ppermute(send, 'core', swap_core)]
    all_to_all x2 -> x0, waiting for transfers between devices: 14 us -> none  [exchange(): return lax.all_to_all(value, axes, 0, 0, tiled=True)]
    all_to_all x2 -> x0, starting transfers between devices: 11.8 us -> none  [exchange(): return lax.all_to_all(value, axes, 0, 0, tiled=True)]
    all_to_all x3, blocking collectives: 37.1 us -> 47.4 us  [exchange(): return lax.all_to_all(value, axes, 0, 0, tiled=True)]
    ppermute x6 -> x1, waiting for transfers between devices: 9.07 us -> 0.96 us  [shards(): got = lax.ppermute(send, 'core', swap_core)]
    unnamed x10 -> x6, local copies, waits for them, and re-layouts: 3.61 us -> 0.01 us
    ppermute x1, waiting for transfers between devices: 0.01 us -> 1.7 us  [shards(): other = lax.ppermute(mine, 'core', swap_core)]
  transfers between devices with their start and end apart: 9 -> 2, of which waited for: 5 -> 2; matrix products, arithmetic and copies ran while one was open for 0% -> 0% of each run, Pallas kernels for 1% -> 0%
where the time goes in v3:
time: 109 us; the launch traced here: 108 us
  blocking collectives  83.5 us (77%)
  starting transfers between devices  12.5 us (11%)
  Pallas kernels  8.91 us (8%)
  waiting for transfers between devices  2.66 us (2%)
    all_to_all x3, blocking collectives, exchange(): return lax.all_to_all(value, axes, 0, 0, tiled=True)  47.4 us
    all_gather x1, blocking collectives, shards(): ring = lax.all_gather(packed, RING, axis=0, tiled=True)  36.1 us
    ppermute x1, starting transfers between devices, shards(): got = lax.ppermute(send, 'core', swap_core)  9.24 us
    pallas_call x6, Pallas kernels, call(): pl.pallas_call(body, out_shape=outs, in_specs=specs, out_specs=[vmem] * l...  8.91 us
    ppermute x1, starting transfers between devices, shards(): other = lax.ppermute(mine, 'core', swap_core)  3.27 us
  transfers between devices with their start and end apart: 2, of which 2 were waited for; matrix products, arithmetic and copies ran while one was open for 0% of the time, Pallas kernels for 0%

profile of v3, /device:TPU:1, one launch (start us, length us, event | category | flops | bytes accessed | tf_op | source)
XLA Modules:
  0.0 108.3 jit_solution(6028528198847879559)
XLA Ops:
  0.0 1.6 %shard_map.55 = bf16[32,976]{1,0:T(8,128)(2,1)} custom-call(f32[64,200]{1,0:T(8,128)} %bitcast.10, bf16[32,1024]{1,0:T(8,128)(2,1)} %bitcast.13), custom_call_target="tpu_custom_call" | custom-call | tf_op jit(solution)/shard_map/pallas_call | solution.py:188
  1.7 36.1 %all_gather.3 = bf16[512,976]{1,0:T(8,128)(2,1)S(1)} all-gather(bf16[32,976]{1,0:T(8,128)(2,1)} %shard_map.55), channel_id=1, replica_groups=mesh['zl'=8,'core'=2,'y'=4,'x'=4,'zh'=2] {'zh','zl'}, dimensions={0}, use_global_device_ids=true | all-gather | bytes 1061888 | tf_op jit(solution)/shard_map/all_gather | solution.py:213
  37.7 0.0 copy-start
  37.7 0.0 copy-start.2
  37.7 0.2 shard_map.56
  37.9 9.2 %collective-permute-start = (bf16[8,32,1152]{2,1,0:T(8,128)(2,1)S(1)}, bf16[8,32,1152]{2,1,0:T(8,128)(2,1)S(1)}, u32[]{:S(2)}, u32[]{:S(2)}) collective-permute-start(bf16[8,32,1152]{2,1,0:T(8,128)(2,1)S(1)} %get-tuple-element.10), channel_id=1, source_target_pairs={{0,32},{32,0},{1,33},{33,1},{2,34},{34,2},{3,35},{35,3},{4,36},{36... | collective-permute-start | bytes 1769480 | tf_op jit(solution)/shard_map/ppermute | solution.py:216
  47.8 1.0 collective-permute-done.got_ref
  48.8 0.0 copy-done
  48.8 0.0 copy-done.2
  48.8 1.1 %shard_map.57 = (bf16[1024,256]{1,0:T(8,128)(2,1)S(1)}, f32[16,16,128]{2,1,0:T(8,128)S(1)}) custom-call(f32[1,1]{1,0:T(1,128)S(6)} %copy.6.field_ref, bf16[8,32,1152]{2,1,0:T(8,128)(2,1)S(1)} %get-tuple-element.9.own_ref, bf16[8,32,1152]{2,1,0:T(8,128)(2,1)S(1)} %collective-permute-done.got_ref, f32[200,200]{1,0:T(8,128)S(1)} %bitcast.12, ...), custom_call_target="tpu_custom_call" | custom-call | tf_op jit(solution)/shard_map/pallas_call | solution.py:188
  49.9 13.4 %all_to_all.15.in_ref = f32[16,16,128]{2,1,0:T(8,128)S(1)} all-to-all(f32[16,16,128]{2,1,0:T(8,128)S(1)} %get-tuple-element.11), channel_id=1, replica_groups=mesh['zl'=8,'core'=2,'y'=4,'x'=4,'zh'=2] {'y','x'}, dimensions={0} | all-to-all | bytes 262144 | tf_op jit(solution)/shard_map/all_to_all | solution.py:203
  63.3 18.5 %all_to_all.16.in_ref = f32[16,16,128]{2,1,0:T(8,128)S(1)} all-to-all(f32[16,16,128]{2,1,0:T(8,128)S(1)} %shard_map.58), channel_id=1, replica_groups=mesh['zl'=8,'core'=2,'y'=4,'x'=4,'zh'=2] {'zl','core'}, dimensions={0} | all-to-all | bytes 262144 | tf_op jit(solution)/shard_map/all_to_all | solution.py:203
  81.9 1.6 %shard_map.59 = bf16[512,640]{1,0:T(8,128)(2,1)S(1)} custom-call(f32[16,16,128]{2,1,0:T(8,128)S(1)} %all_to_all.16.in_ref, bf16[8,32,1152]{2,1,0:T(8,128)(2,1)S(1)} %get-tuple-element.9.own_ref, bf16[8,32,1152]{2,1,0:T(8,128)(2,1)S(1)} %collective-permute-done.got_ref), custom_call_target="tpu_custom_call" | custom-call | tf_op jit(solution)/shard_map/pallas_call | solution.py:188
  83.5 0.0 copy-start.1
  83.5 15.4 %all_to_all.17.mine_ref = bf16[16,32,640]{2,1,0:T(8,128)(2,1)S(1)} all-to-all(bf16[16,32,640]{2,1,0:T(8,128)(2,1)S(1)} %bitcast.8), channel_id=1, replica_groups=mesh['zl'=8,'core'=2,'y'=4,'x'=4,'zh'=2] {'y','x'}, dimensions={0} | all-to-all | bytes 1310720 | tf_op jit(solution)/shard_map/all_to_all | solution.py:203
  99.0 3.3 %collective-permute-start.1 = (bf16[16,32,640]{2,1,0:T(8,128)(2,1)S(1)}, bf16[16,32,640]{2,1,0:T(8,128)(2,1)S(1)}, u32[]{:S(2)}, u32[]{:S(2)}) collective-permute-start(bf16[16,32,640]{2,1,0:T(8,128)(2,1)S(1)} %all_to_all.17.mine_ref), channel_id=1, source_target_pairs={{0,32},{32,0},{1,33},{33,1},{2,34},{34,2},{3,35},{35,3},{4,36},{36... | collective-permute-start | bytes 1966088 | tf_op jit(solution)/shard_map/ppermute | solution.py:227
  102.3 1.7 %collective-permute-done.1.other_ref = bf16[16,32,640]{2,1,0:T(8,128)(2,1)S(1)} collective-permute-done((bf16[16,32,640]{2,1,0:T(8,128)(2,1)S(1)}, bf16[16,32,640]{2,1,0:T(8,128)(2,1)S(1)}, u32[]{:S(2)}, u32[]{:S(2)}) %collective-permute-start.1) | collective-permute-done | bytes 655392 | tf_op jit(solution)/shard_map/ppermute | solution.py:227
  104.0 0.0 copy-done.1
  104.0 4.3 %shard_map.60 = f32[64,200]{1,0:T(8,128)} custom-call(f32[64,200]{1,0:T(8,128)S(1)} %bitcast.11, bf16[16,32,640]{2,1,0:T(8,128)(2,1)S(1)} %all_to_all.17.mine_ref, bf16[16,32,640]{2,1,0:T(8,128)(2,1)S(1)} %collective-permute-done.1.other_ref, bf16[1024,256]{1,0:T(8,128)(2,1)S(1)} %get-tuple-element.12.first_ref), custom_call_target="tpu_custom_call" | custom-call | tf_op jit(solution)/shard_map/pallas_call | solution.py:188
  (1 shorter events, 0.0 us)
Async XLA Ops:
  37.7 11.0 %copy-start = (bf16[1,200,1024]{2,1,0:T(8,128)(2,1)S(1)}, bf16[1,200,1024]{2,1,0:T(8,128)(2,1)}, u32[]{:S(2)}) copy-start(bf16[1,200,1024]{2,1,0:T(8,128)(2,1)} %param.7) | copy-start | bytes 1228804
  37.7 11.0 %copy-start.2 = (f32[1,200,200]{2,1,0:T(8,128)S(1)}, f32[1,200,200]{2,1,0:T(8,128)}, u32[]{:S(2)}) copy-start(f32[1,200,200]{2,1,0:T(8,128)} %param.6) | copy-start | bytes 480004
  37.9 10.9 %collective-permute-start = (bf16[8,32,1152]{2,1,0:T(8,128)(2,1)S(1)}, bf16[8,32,1152]{2,1,0:T(8,128)(2,1)S(1)}, u32[]{:S(2)}, u32[]{:S(2)}) collective-permute-start(bf16[8,32,1152]{2,1,0:T(8,128)(2,1)S(1)} %get-tuple-element.10), channel_id=1, source_target_pairs={{0,32},{32,0},{1,33},{33,1},{2,34},{34,2},{3,35},{35,3},{4,36},{36... | collective-permute-start | bytes 1769480 | tf_op jit(solution)/shard_map/ppermute | solution.py:216
  83.5 20.4 %copy-start.1 = (f32[1,64,200]{2,1,0:T(8,128)S(1)}, f32[1,64,200]{2,1,0:T(8,128)}, u32[]{:S(2)}) copy-start(f32[1,64,200]{2,1,0:T(8,128)} %param.5) | copy-start | bytes 153604
  99.0 5.0 %collective-permute-start.1 = (bf16[16,32,640]{2,1,0:T(8,128)(2,1)S(1)}, bf16[16,32,640]{2,1,0:T(8,128)(2,1)S(1)}, u32[]{:S(2)}, u32[]{:S(2)}) collective-permute-start(bf16[16,32,640]{2,1,0:T(8,128)(2,1)S(1)} %all_to_all.17.mine_ref), channel_id=1, source_target_pairs={{0,32},{32,0},{1,33},{33,1},{2,34},{34,2},{3,35},{35,3},{4,36},{36... | collective-permute-start | bytes 1966088 | tf_op jit(solution)/shard_map/ppermute | solution.py:227

commit v4 on v3

--- a/solution.py
+++ b/solution.py
@@ -99,21 +99,20 @@
     diagonal = jnp.where(iota((200, 256), 0) == iota((200, 256), 1), product, 0.0)
     raw_bias = jnp.sum(jnp.sum(diagonal, axis=0, keepdims=True), axis=1, keepdims=True)
     shifted = field_scale * (field_ref[0, 0] - jnp.clip(raw_bias, -1.0, 1.0))
-    here = (iota((16, 128), 0) == chol_index()) & (iota((16, 128), 1) == plane_index())
-    tile = jnp.where(here, shifted, 0.0)
+    row = jnp.where(iota((1, 128), 1) == plane_index(), shifted, 0.0)
     for j in range(16):
-        out_ref[j] = tile
+        out_ref[j] = row
 
 
 def sum_kernel(in_ref, out_ref):
-    tile = jnp.sum(in_ref[...], axis=0)
+    row = jnp.sum(in_ref[...], axis=0)
     for j in range(16):
-        out_ref[j] = tile
+        out_ref[j] = row
 
 
 def operator_kernel(in_ref, own_ref, got_ref, out_ref):
     k = lax.axis_index("core")
-    shifted = jnp.sum(in_ref[...], axis=0)
+    shifted = in_ref[:, 0, :]
     by_walker = jnp.concatenate([shifted, jnp.zeros((112, 128), f32)], axis=0).T
     high = by_walker.astype(bf16)
     rest = (by_walker - high.astype(f32)).astype(bf16)
@@ -215,12 +214,12 @@
     swap_core = [(0, 1), (1, 0)]
     got = lax.ppermute(send, "core", swap_core)
     first, partial = call(
-        bias_kernel, [shape((1024, 256), bf16), shape((16, 16, 128), f32)],
+        bias_kernel, [shape((1024, 256), bf16), shape((16, 1, 128), f32)],
         fields, own, got, inverse_intersection[0], half_rotated[0],
         scratch=[pltpu.VMEM((256, 256), bf16), pltpu.VMEM((256, 256), bf16)], smem=1,
     )
     in_plane = exchange(partial, PLANE)
-    summed = call(sum_kernel, shape((16, 16, 128), f32), in_plane)
+    summed = call(sum_kernel, shape((16, 1, 128), f32), in_plane)
     everywhere = exchange(summed, CHOL)
     pieces = call(operator_kernel, shape((512, 640), bf16), everywhere, own, got)
     mine = exchange(pieces.reshape(16, 32, 640), PLANE)

time: 109 us -> 106 us (0.972)
  blocking collectives: 83.5 us -> 79.8 us
    all_to_all x3, blocking collectives: 47.4 us -> 43.7 us  [exchange(): return lax.all_to_all(value, axes, 0, 0, tiled=True)]
where the time goes in v4:
time: 106 us; the launch traced here: 105 us
  blocking collectives  79.8 us (75%)
  starting transfers between devices  13.3 us (13%)
  Pallas kernels  8.89 us (8%)
  waiting for transfers between devices  2.66 us (3%)
    all_to_all x3, blocking collectives, exchange(): return lax.all_to_all(value, axes, 0, 0, tiled=True)  43.7 us
    all_gather x1, blocking collectives, shards(): ring = lax.all_gather(packed, RING, axis=0, tiled=True)  36.1 us
    ppermute x1, starting transfers between devices, shards(): got = lax.ppermute(send, 'core', swap_core)  9.24 us
    pallas_call x6, Pallas kernels, call(): pl.pallas_call(body, out_shape=outs, in_specs=specs, out_specs=[vmem] * l...  8.89 us
    ppermute x1, starting transfers between devices, shards(): other = lax.ppermute(mine, 'core', swap_core)  4.05 us
  transfers between devices with their start and end apart: 2, of which 2 were waited for; matrix products, arithmetic and copies ran while one was open for 0% of the time, Pallas kernels for 0%

profile of v4, /device:TPU:1, one launch (start us, length us, event | category | flops | bytes accessed | tf_op | source)
XLA Modules:
  0.0 105.4 jit_solution(12215825081275909584)
XLA Ops:
  0.0 1.6 %shard_map.55 = bf16[32,976]{1,0:T(8,128)(2,1)} custom-call(f32[64,200]{1,0:T(8,128)} %bitcast.10, bf16[32,1024]{1,0:T(8,128)(2,1)} %bitcast.13), custom_call_target="tpu_custom_call" | custom-call | tf_op jit(solution)/shard_map/pallas_call | solution.py:187
  1.7 36.1 %all_gather.3 = bf16[512,976]{1,0:T(8,128)(2,1)S(1)} all-gather(bf16[32,976]{1,0:T(8,128)(2,1)} %shard_map.55), channel_id=1, replica_groups=mesh['zl'=8,'core'=2,'y'=4,'x'=4,'zh'=2] {'zh','zl'}, dimensions={0}, use_global_device_ids=true | all-gather | bytes 1061888 | tf_op jit(solution)/shard_map/all_gather | solution.py:212
  37.7 0.0 copy-start
  37.7 0.0 copy-start.2
  37.7 0.2 shard_map.56
  37.9 9.2 %collective-permute-start = (bf16[8,32,1152]{2,1,0:T(8,128)(2,1)S(1)}, bf16[8,32,1152]{2,1,0:T(8,128)(2,1)S(1)}, u32[]{:S(2)}, u32[]{:S(2)}) collective-permute-start(bf16[8,32,1152]{2,1,0:T(8,128)(2,1)S(1)} %get-tuple-element.10), channel_id=1, source_target_pairs={{0,32},{32,0},{1,33},{33,1},{2,34},{34,2},{3,35},{35,3},{4,36},{36... | collective-permute-start | bytes 1769480 | tf_op jit(solution)/shard_map/ppermute | solution.py:215
  47.8 1.0 collective-permute-done.got_ref
  48.8 0.0 copy-done
  48.8 0.0 copy-done.2
  48.8 1.1 %shard_map.57 = (bf16[1024,256]{1,0:T(8,128)(2,1)S(1)}, f32[16,1,128]{2,1,0:T(1,128)S(1)}) custom-call(f32[1,1]{1,0:T(1,128)S(6)} %copy.6.field_ref, bf16[8,32,1152]{2,1,0:T(8,128)(2,1)S(1)} %get-tuple-element.9.own_ref, bf16[8,32,1152]{2,1,0:T(8,128)(2,1)S(1)} %collective-permute-done.got_ref, f32[200,200]{1,0:T(8,128)S(1)} %bitcast.12, ...), custom_call_target="tpu_custom_call" | custom-call | tf_op jit(solution)/shard_map/pallas_call | solution.py:187
  49.9 13.0 %all_to_all.15.in_ref = f32[16,1,128]{2,1,0:T(1,128)S(1)} all-to-all(f32[16,1,128]{2,1,0:T(1,128)S(1)} %get-tuple-element.11), channel_id=1, replica_groups=mesh['zl'=8,'core'=2,'y'=4,'x'=4,'zh'=2] {'y','x'}, dimensions={0} | all-to-all | bytes 16384 | tf_op jit(solution)/shard_map/all_to_all | solution.py:202
  62.9 16.2 %all_to_all.16.in_ref = f32[16,1,128]{2,1,0:T(1,128)S(1)} all-to-all(f32[16,1,128]{2,1,0:T(1,128)S(1)} %shard_map.58), channel_id=1, replica_groups=mesh['zl'=8,'core'=2,'y'=4,'x'=4,'zh'=2] {'zl','core'}, dimensions={0} | all-to-all | bytes 16384 | tf_op jit(solution)/shard_map/all_to_all | solution.py:202
  79.1 1.6 %shard_map.59 = bf16[512,640]{1,0:T(8,128)(2,1)S(1)} custom-call(f32[16,1,128]{2,1,0:T(1,128)S(1)} %all_to_all.16.in_ref, bf16[8,32,1152]{2,1,0:T(8,128)(2,1)S(1)} %get-tuple-element.9.own_ref, bf16[8,32,1152]{2,1,0:T(8,128)(2,1)S(1)} %collective-permute-done.got_ref), custom_call_target="tpu_custom_call" | custom-call | tf_op jit(solution)/shard_map/pallas_call | solution.py:187
  80.7 0.0 copy-start.1
  80.8 14.6 %all_to_all.17.mine_ref = bf16[16,32,640]{2,1,0:T(8,128)(2,1)S(1)} all-to-all(bf16[16,32,640]{2,1,0:T(8,128)(2,1)S(1)} %bitcast.8), channel_id=1, replica_groups=mesh['zl'=8,'core'=2,'y'=4,'x'=4,'zh'=2] {'y','x'}, dimensions={0} | all-to-all | bytes 1310720 | tf_op jit(solution)/shard_map/all_to_all | solution.py:202
  95.3 4.1 %collective-permute-start.1 = (bf16[16,32,640]{2,1,0:T(8,128)(2,1)S(1)}, bf16[16,32,640]{2,1,0:T(8,128)(2,1)S(1)}, u32[]{:S(2)}, u32[]{:S(2)}) collective-permute-start(bf16[16,32,640]{2,1,0:T(8,128)(2,1)S(1)} %all_to_all.17.mine_ref), channel_id=1, source_target_pairs={{0,32},{32,0},{1,33},{33,1},{2,34},{34,2},{3,35},{35,3},{4,36},{36... | collective-permute-start | bytes 1966088 | tf_op jit(solution)/shard_map/ppermute | solution.py:226
  99.4 1.7 %collective-permute-done.1.other_ref = bf16[16,32,640]{2,1,0:T(8,128)(2,1)S(1)} collective-permute-done((bf16[16,32,640]{2,1,0:T(8,128)(2,1)S(1)}, bf16[16,32,640]{2,1,0:T(8,128)(2,1)S(1)}, u32[]{:S(2)}, u32[]{:S(2)}) %collective-permute-start.1) | collective-permute-done | bytes 655392 | tf_op jit(solution)/shard_map/ppermute | solution.py:226
  101.1 0.0 copy-done.1
  101.1 4.3 %shard_map.60 = f32[64,200]{1,0:T(8,128)} custom-call(f32[64,200]{1,0:T(8,128)S(1)} %bitcast.11, bf16[16,32,640]{2,1,0:T(8,128)(2,1)S(1)} %all_to_all.17.mine_ref, bf16[16,32,640]{2,1,0:T(8,128)(2,1)S(1)} %collective-permute-done.1.other_ref, bf16[1024,256]{1,0:T(8,128)(2,1)S(1)} %get-tuple-element.12.first_ref), custom_call_target="tpu_custom_call" | custom-call | tf_op jit(solution)/shard_map/pallas_call | solution.py:187
  (1 shorter events, 0.0 us)
Async XLA Ops:
  37.7 11.0 %copy-start = (bf16[1,200,1024]{2,1,0:T(8,128)(2,1)S(1)}, bf16[1,200,1024]{2,1,0:T(8,128)(2,1)}, u32[]{:S(2)}) copy-start(bf16[1,200,1024]{2,1,0:T(8,128)(2,1)} %param.7) | copy-start | bytes 1228804
  37.7 11.0 %copy-start.2 = (f32[1,200,200]{2,1,0:T(8,128)S(1)}, f32[1,200,200]{2,1,0:T(8,128)}, u32[]{:S(2)}) copy-start(f32[1,200,200]{2,1,0:T(8,128)} %param.6) | copy-start | bytes 480004
  37.9 10.9 %collective-permute-start = (bf16[8,32,1152]{2,1,0:T(8,128)(2,1)S(1)}, bf16[8,32,1152]{2,1,0:T(8,128)(2,1)S(1)}, u32[]{:S(2)}, u32[]{:S(2)}) collective-permute-start(bf16[8,32,1152]{2,1,0:T(8,128)(2,1)S(1)} %get-tuple-element.10), channel_id=1, source_target_pairs={{0,32},{32,0},{1,33},{33,1},{2,34},{34,2},{3,35},{35,3},{4,36},{36... | collective-permute-start | bytes 1769480 | tf_op jit(solution)/shard_map/ppermute | solution.py:215
  80.7 20.4 %copy-start.1 = (f32[1,64,200]{2,1,0:T(8,128)S(1)}, f32[1,64,200]{2,1,0:T(8,128)}, u32[]{:S(2)}) copy-start(f32[1,64,200]{2,1,0:T(8,128)} %param.5) | copy-start | bytes 153604
  95.3 5.8 %collective-permute-start.1 = (bf16[16,32,640]{2,1,0:T(8,128)(2,1)S(1)}, bf16[16,32,640]{2,1,0:T(8,128)(2,1)S(1)}, u32[]{:S(2)}, u32[]{:S(2)}) collective-permute-start(bf16[16,32,640]{2,1,0:T(8,128)(2,1)S(1)} %all_to_all.17.mine_ref), channel_id=1, source_target_pairs={{0,32},{32,0},{1,33},{33,1},{2,34},{34,2},{3,35},{35,3},{4,36},{36... | collective-permute-start | bytes 1966088 | tf_op jit(solution)/shard_map/ppermute | solution.py:226

commit v5 on v4

--- a/solution.py
+++ b/solution.py
@@ -99,7 +99,7 @@
     diagonal = jnp.where(iota((200, 256), 0) == iota((200, 256), 1), product, 0.0)
     raw_bias = jnp.sum(jnp.sum(diagonal, axis=0, keepdims=True), axis=1, keepdims=True)
     shifted = field_scale * (field_ref[0, 0] - jnp.clip(raw_bias, -1.0, 1.0))
-    row = jnp.where(iota((1, 128), 1) == plane_index(), shifted, 0.0)
+    row = jnp.where(iota((1, 128), 1) == chol_index(), shifted, 0.0)
     for j in range(16):
         out_ref[j] = row
 
@@ -112,8 +112,7 @@
 
 def operator_kernel(in_ref, own_ref, got_ref, out_ref):
     k = lax.axis_index("core")
-    shifted = in_ref[:, 0, :]
-    by_walker = jnp.concatenate([shifted, jnp.zeros((112, 128), f32)], axis=0).T
+    by_walker = jnp.concatenate([in_ref[:, 0, :], jnp.zeros((112, 128), f32)], axis=0)
     high = by_walker.astype(bf16)
     rest = (by_walker - high.astype(f32)).astype(bf16)
     g, q = iota((128, 512), 0), iota((128, 512), 1) >> 5
@@ -218,9 +217,9 @@
         fields, own, got, inverse_intersection[0], half_rotated[0],
         scratch=[pltpu.VMEM((256, 256), bf16), pltpu.VMEM((256, 256), bf16)], smem=1,
     )
-    in_plane = exchange(partial, PLANE)
-    summed = call(sum_kernel, shape((16, 1, 128), f32), in_plane)
-    everywhere = exchange(summed, CHOL)
+    along_z = exchange(partial, CHOL)
+    summed = call(sum_kernel, shape((16, 1, 128), f32), along_z)
+    everywhere = exchange(summed, PLANE)
     pieces = call(operator_kernel, shape((512, 640), bf16), everywhere, own, got)
     mine = exchange(pieces.reshape(16, 32, 640), PLANE)
     other = lax.ppermute(mine, "core", swap_core)

time: 106 us -> 104 us (0.981)
  blocking collectives: 79.8 us -> 77.3 us
  starting transfers between devices: 13.3 us -> 14.4 us
    all_to_all x3, blocking collectives: 43.7 us -> 41.2 us  [exchange(): return lax.all_to_all(value, axes, 0, 0, tiled=True)]
    ppermute x1, starting transfers between devices: 4.05 us -> 5.16 us  [shards(): other = lax.ppermute(mine, 'core', swap_core)]
where the time goes in v5:
time: 104 us
  blocking collectives  77.3 us (74%)
  starting transfers between devices  14.4 us (14%)
  Pallas kernels  8.85 us (9%)
  waiting for transfers between devices  2.66 us (3%)
    all_to_all x3, blocking collectives, exchange(): return lax.all_to_all(value, axes, 0, 0, tiled=True)  41.2 us
    all_gather x1, blocking collectives, shards(): ring = lax.all_gather(packed, RING, axis=0, tiled=True)  36.1 us
    ppermute x1, starting transfers between devices, shards(): got = lax.ppermute(send, 'core', swap_core)  9.24 us
    pallas_call x6, Pallas kernels, call(): pl.pallas_call(body, out_shape=outs, in_specs=specs, out_specs=[vmem] * l...  8.85 us
    ppermute x1, starting transfers between devices, shards(): other = lax.ppermute(mine, 'core', swap_core)  5.16 us
  transfers between devices with their start and end apart: 2, of which 2 were waited for; matrix products, arithmetic and copies ran while one was open for 0% of the time, Pallas kernels for 0%

profile of v5, /device:TPU:1, one launch (start us, length us, event | category | flops | bytes accessed | tf_op | source)
XLA Modules:
  0.0 103.9 jit_solution(13907513382125288331)
XLA Ops:
  0.0 1.6 %shard_map.55 = bf16[32,976]{1,0:T(8,128)(2,1)} custom-call(f32[64,200]{1,0:T(8,128)} %bitcast.10, bf16[32,1024]{1,0:T(8,128)(2,1)} %bitcast.13), custom_call_target="tpu_custom_call" | custom-call | tf_op jit(solution)/shard_map/pallas_call | solution.py:186
  1.7 36.1 %all_gather.3 = bf16[512,976]{1,0:T(8,128)(2,1)S(1)} all-gather(bf16[32,976]{1,0:T(8,128)(2,1)} %shard_map.55), channel_id=1, replica_groups=mesh['zl'=8,'core'=2,'y'=4,'x'=4,'zh'=2] {'zh','zl'}, dimensions={0}, use_global_device_ids=true | all-gather | bytes 1061888 | tf_op jit(solution)/shard_map/all_gather | solution.py:211
  37.7 0.0 copy-start
  37.7 0.0 copy-start.2
  37.7 0.2 shard_map.56
  37.9 9.2 %collective-permute-start = (bf16[8,32,1152]{2,1,0:T(8,128)(2,1)S(1)}, bf16[8,32,1152]{2,1,0:T(8,128)(2,1)S(1)}, u32[]{:S(2)}, u32[]{:S(2)}) collective-permute-start(bf16[8,32,1152]{2,1,0:T(8,128)(2,1)S(1)} %get-tuple-element.10), channel_id=1, source_target_pairs={{0,32},{32,0},{1,33},{33,1},{2,34},{34,2},{3,35},{35,3},{4,36},{36... | collective-permute-start | bytes 1769480 | tf_op jit(solution)/shard_map/ppermute | solution.py:214
  47.8 1.0 collective-permute-done.got_ref
  48.8 0.0 copy-done
  48.8 0.0 copy-done.2
  48.8 1.1 %shard_map.57 = (bf16[1024,256]{1,0:T(8,128)(2,1)S(1)}, f32[16,1,128]{2,1,0:T(1,128)S(1)}) custom-call(f32[1,1]{1,0:T(1,128)S(6)} %copy.6.field_ref, bf16[8,32,1152]{2,1,0:T(8,128)(2,1)S(1)} %get-tuple-element.9.own_ref, bf16[8,32,1152]{2,1,0:T(8,128)(2,1)S(1)} %collective-permute-done.got_ref, f32[200,200]{1,0:T(8,128)S(1)} %bitcast.12, ...), custom_call_target="tpu_custom_call" | custom-call | tf_op jit(solution)/shard_map/pallas_call | solution.py:186
  49.9 14.8 %all_to_all.15.in_ref = f32[16,1,128]{2,1,0:T(1,128)S(1)} all-to-all(f32[16,1,128]{2,1,0:T(1,128)S(1)} %get-tuple-element.11), channel_id=1, replica_groups=mesh['zl'=8,'core'=2,'y'=4,'x'=4,'zh'=2] {'zl','core'}, dimensions={0} | all-to-all | bytes 16384 | tf_op jit(solution)/shard_map/all_to_all | solution.py:201
  64.7 13.0 %all_to_all.16.in_ref = f32[16,1,128]{2,1,0:T(1,128)S(1)} all-to-all(f32[16,1,128]{2,1,0:T(1,128)S(1)} %shard_map.58), channel_id=1, replica_groups=mesh['zl'=8,'core'=2,'y'=4,'x'=4,'zh'=2] {'y','x'}, dimensions={0} | all-to-all | bytes 16384 | tf_op jit(solution)/shard_map/all_to_all | solution.py:201
  77.7 1.6 %shard_map.59 = bf16[512,640]{1,0:T(8,128)(2,1)S(1)} custom-call(f32[16,1,128]{2,1,0:T(1,128)S(1)} %all_to_all.16.in_ref, bf16[8,32,1152]{2,1,0:T(8,128)(2,1)S(1)} %get-tuple-element.9.own_ref, bf16[8,32,1152]{2,1,0:T(8,128)(2,1)S(1)} %collective-permute-done.got_ref), custom_call_target="tpu_custom_call" | custom-call | tf_op jit(solution)/shard_map/pallas_call | solution.py:186
  79.3 0.0 copy-start.1
  79.3 13.5 %all_to_all.17.mine_ref = bf16[16,32,640]{2,1,0:T(8,128)(2,1)S(1)} all-to-all(bf16[16,32,640]{2,1,0:T(8,128)(2,1)S(1)} %bitcast.8), channel_id=1, replica_groups=mesh['zl'=8,'core'=2,'y'=4,'x'=4,'zh'=2] {'y','x'}, dimensions={0} | all-to-all | bytes 1310720 | tf_op jit(solution)/shard_map/all_to_all | solution.py:201
  92.8 5.2 %collective-permute-start.1 = (bf16[16,32,640]{2,1,0:T(8,128)(2,1)S(1)}, bf16[16,32,640]{2,1,0:T(8,128)(2,1)S(1)}, u32[]{:S(2)}, u32[]{:S(2)}) collective-permute-start(bf16[16,32,640]{2,1,0:T(8,128)(2,1)S(1)} %all_to_all.17.mine_ref), channel_id=1, source_target_pairs={{0,32},{32,0},{1,33},{33,1},{2,34},{34,2},{3,35},{35,3},{4,36},{36... | collective-permute-start | bytes 1966088 | tf_op jit(solution)/shard_map/ppermute | solution.py:225
  97.9 1.7 %collective-permute-done.1.other_ref = bf16[16,32,640]{2,1,0:T(8,128)(2,1)S(1)} collective-permute-done((bf16[16,32,640]{2,1,0:T(8,128)(2,1)S(1)}, bf16[16,32,640]{2,1,0:T(8,128)(2,1)S(1)}, u32[]{:S(2)}, u32[]{:S(2)}) %collective-permute-start.1) | collective-permute-done | bytes 655392 | tf_op jit(solution)/shard_map/ppermute | solution.py:225
  99.6 0.0 copy-done.1
  99.6 4.3 %shard_map.60 = f32[64,200]{1,0:T(8,128)} custom-call(f32[64,200]{1,0:T(8,128)S(1)} %bitcast.11, bf16[16,32,640]{2,1,0:T(8,128)(2,1)S(1)} %all_to_all.17.mine_ref, bf16[16,32,640]{2,1,0:T(8,128)(2,1)S(1)} %collective-permute-done.1.other_ref, bf16[1024,256]{1,0:T(8,128)(2,1)S(1)} %get-tuple-element.12.first_ref), custom_call_target="tpu_custom_call" | custom-call | tf_op jit(solution)/shard_map/pallas_call | solution.py:186
  (1 shorter events, 0.0 us)
Async XLA Ops:
  37.7 11.0 %copy-start = (bf16[1,200,1024]{2,1,0:T(8,128)(2,1)S(1)}, bf16[1,200,1024]{2,1,0:T(8,128)(2,1)}, u32[]{:S(2)}) copy-start(bf16[1,200,1024]{2,1,0:T(8,128)(2,1)} %param.7) | copy-start | bytes 1228804
  37.7 11.0 %copy-start.2 = (f32[1,200,200]{2,1,0:T(8,128)S(1)}, f32[1,200,200]{2,1,0:T(8,128)}, u32[]{:S(2)}) copy-start(f32[1,200,200]{2,1,0:T(8,128)} %param.6) | copy-start | bytes 480004
  37.9 10.9 %collective-permute-start = (bf16[8,32,1152]{2,1,0:T(8,128)(2,1)S(1)}, bf16[8,32,1152]{2,1,0:T(8,128)(2,1)S(1)}, u32[]{:S(2)}, u32[]{:S(2)}) collective-permute-start(bf16[8,32,1152]{2,1,0:T(8,128)(2,1)S(1)} %get-tuple-element.10), channel_id=1, source_target_pairs={{0,32},{32,0},{1,33},{33,1},{2,34},{34,2},{3,35},{35,3},{4,36},{36... | collective-permute-start | bytes 1769480 | tf_op jit(solution)/shard_map/ppermute | solution.py:214
  79.3 20.4 %copy-start.1 = (f32[1,64,200]{2,1,0:T(8,128)S(1)}, f32[1,64,200]{2,1,0:T(8,128)}, u32[]{:S(2)}) copy-start(f32[1,64,200]{2,1,0:T(8,128)} %param.5) | copy-start | bytes 153604
  92.8 6.9 %collective-permute-start.1 = (bf16[16,32,640]{2,1,0:T(8,128)(2,1)S(1)}, bf16[16,32,640]{2,1,0:T(8,128)(2,1)S(1)}, u32[]{:S(2)}, u32[]{:S(2)}) collective-permute-start(bf16[16,32,640]{2,1,0:T(8,128)(2,1)S(1)} %all_to_all.17.mine_ref), channel_id=1, source_target_pairs={{0,32},{32,0},{1,33},{33,1},{2,34},{34,2},{3,35},{35,3},{4,36},{36... | collective-permute-start | bytes 1966088 | tf_op jit(solution)/shard_map/ppermute | solution.py:225

commit v6 on v5

--- a/solution.py
+++ b/solution.py
@@ -137,7 +137,7 @@
         out_ref[rows, :] = value.astype(bf16)
 
 
-def taylor_kernel(orb_ref, mine_ref, other_ref, first_ref, out_ref, op, tail, term_a, term_b):
+def taylor_kernel(orb_ref, mine_ref, other_ref, first_ref, out_ref, op, tail):
     k = lax.axis_index("core")
     for p in range(16):
         here = pl.multiple_of(64 * p + 32 * k, 32)
@@ -164,16 +164,18 @@
         op[128 * j:128 * j + 128, 128 * i:128 * i + 128] = block.T.astype(bf16)
     own = pl.multiple_of(chol_index() * 64, 64)
     own_rows = op[pl.ds(own, 64), :]
-    total = jnp.zeros((64, 256), f32)
-    now, later, spare = first_ref, term_a, term_b
-    for degree in range(1, TAYLOR + 1):
-        term = now[...]
-        total += jnp.dot(own_rows, term, preferred_element_type=f32) * (1.0 / degree)
-        if degree < TAYLOR:
-            for i in range(4):
-                image = jnp.dot(op[256 * i:256 * i + 256, :], term, preferred_element_type=f32)
-                later[256 * i:256 * i + 256, :] = (image * (1.0 / degree)).astype(bf16)
-            now, later, spare = later, spare, later
+    power, share = own_rows, 1.0
+    series = power.astype(f32)
+    for degree in range(2, TAYLOR + 1):
+        product = jnp.dot(power, op[...], preferred_element_type=f32)
+        share = share / degree
+        series += product * share
+        power = product.astype(bf16)
+    high = series.astype(bf16)
+    rest = (series - high.astype(f32)).astype(bf16)
+    first = first_ref[...]
+    total = jnp.dot(rest, first, preferred_element_type=f32)
+    total += jnp.dot(high, first, preferred_element_type=f32)
     out_ref[...] = orb_ref[...] + total[:, :200]
 
 
@@ -225,8 +227,7 @@
     other = lax.ppermute(mine, "core", swap_core)
     out = call(
         taylor_kernel, shape((64, 200), f32), orb, mine, other, first,
-        scratch=[pltpu.VMEM((1024, 1024), bf16), pltpu.VMEM((1024, 128), f32),
-                 pltpu.VMEM((1024, 256), bf16), pltpu.VMEM((1024, 256), bf16)],
+        scratch=[pltpu.VMEM((1024, 1024), bf16), pltpu.VMEM((1024, 128), f32)],
     )
     return out[None]
 

time: 104 us -> 103 us (level)
  Pallas kernels: 8.85 us -> 7.77 us
    pallas_call x6, Pallas kernels: 8.85 us -> 7.77 us  [call(): pl.pallas_call(body, out_shape=outs, in_specs=specs, out_specs=[vmem] * l...]
where the time goes in v6:
time: 103 us
  blocking collectives  77.3 us (75%)
  starting transfers between devices  14.4 us (14%)
  Pallas kernels  7.77 us (8%)
  waiting for transfers between devices  2.66 us (3%)
    all_to_all x3, blocking collectives, exchange(): return lax.all_to_all(value, axes, 0, 0, tiled=True)  41.2 us
    all_gather x1, blocking collectives, shards(): ring = lax.all_gather(packed, RING, axis=0, tiled=True)  36.1 us
    ppermute x1, starting transfers between devices, shards(): got = lax.ppermute(send, 'core', swap_core)  9.24 us
    pallas_call x6, Pallas kernels, call(): pl.pallas_call(body, out_shape=outs, in_specs=specs, out_specs=[vmem] * l...  7.77 us
    ppermute x1, starting transfers between devices, shards(): other = lax.ppermute(mine, 'core', swap_core)  5.16 us
  transfers between devices with their start and end apart: 2, of which 2 were waited for; matrix products, arithmetic and copies ran while one was open for 0% of the time, Pallas kernels for 0%

profile of v6, /device:TPU:1, one launch (start us, length us, event | category | flops | bytes accessed | tf_op | source)
XLA Modules:
  0.0 102.8 jit_solution(9591380918990752988)
XLA Ops:
  0.0 1.6 %shard_map.55 = bf16[32,976]{1,0:T(8,128)(2,1)} custom-call(f32[64,200]{1,0:T(8,128)} %bitcast.10, bf16[32,1024]{1,0:T(8,128)(2,1)} %bitcast.13), custom_call_target="tpu_custom_call" | custom-call | tf_op jit(solution)/shard_map/pallas_call | solution.py:188
  1.7 36.1 %all_gather.3 = bf16[512,976]{1,0:T(8,128)(2,1)S(1)} all-gather(bf16[32,976]{1,0:T(8,128)(2,1)} %shard_map.55), channel_id=1, replica_groups=mesh['zl'=8,'core'=2,'y'=4,'x'=4,'zh'=2] {'zh','zl'}, dimensions={0}, use_global_device_ids=true | all-gather | bytes 1061888 | tf_op jit(solution)/shard_map/all_gather | solution.py:213
  37.7 0.0 copy-start
  37.7 0.0 copy-start.2
  37.7 0.2 shard_map.56
  37.9 9.2 %collective-permute-start = (bf16[8,32,1152]{2,1,0:T(8,128)(2,1)S(1)}, bf16[8,32,1152]{2,1,0:T(8,128)(2,1)S(1)}, u32[]{:S(2)}, u32[]{:S(2)}) collective-permute-start(bf16[8,32,1152]{2,1,0:T(8,128)(2,1)S(1)} %get-tuple-element.10), channel_id=1, source_target_pairs={{0,32},{32,0},{1,33},{33,1},{2,34},{34,2},{3,35},{35,3},{4,36},{36... | collective-permute-start | bytes 1769480 | tf_op jit(solution)/shard_map/ppermute | solution.py:216
  47.8 1.0 collective-permute-done.got_ref
  48.8 0.0 copy-done
  48.8 0.0 copy-done.2
  48.8 1.1 %shard_map.57 = (bf16[1024,256]{1,0:T(8,128)(2,1)S(1)}, f32[16,1,128]{2,1,0:T(1,128)S(1)}) custom-call(f32[1,1]{1,0:T(1,128)S(6)} %copy.6.field_ref, bf16[8,32,1152]{2,1,0:T(8,128)(2,1)S(1)} %get-tuple-element.9.own_ref, bf16[8,32,1152]{2,1,0:T(8,128)(2,1)S(1)} %collective-permute-done.got_ref, f32[200,200]{1,0:T(8,128)S(1)} %bitcast.12, ...), custom_call_target="tpu_custom_call" | custom-call | tf_op jit(solution)/shard_map/pallas_call | solution.py:188
  49.9 14.8 %all_to_all.15.in_ref = f32[16,1,128]{2,1,0:T(1,128)S(1)} all-to-all(f32[16,1,128]{2,1,0:T(1,128)S(1)} %get-tuple-element.11), channel_id=1, replica_groups=mesh['zl'=8,'core'=2,'y'=4,'x'=4,'zh'=2] {'zl','core'}, dimensions={0} | all-to-all | bytes 16384 | tf_op jit(solution)/shard_map/all_to_all | solution.py:203
  64.7 13.0 %all_to_all.16.in_ref = f32[16,1,128]{2,1,0:T(1,128)S(1)} all-to-all(f32[16,1,128]{2,1,0:T(1,128)S(1)} %shard_map.58), channel_id=1, replica_groups=mesh['zl'=8,'core'=2,'y'=4,'x'=4,'zh'=2] {'y','x'}, dimensions={0} | all-to-all | bytes 16384 | tf_op jit(solution)/shard_map/all_to_all | solution.py:203
  77.7 1.6 %shard_map.59 = bf16[512,640]{1,0:T(8,128)(2,1)S(1)} custom-call(f32[16,1,128]{2,1,0:T(1,128)S(1)} %all_to_all.16.in_ref, bf16[8,32,1152]{2,1,0:T(8,128)(2,1)S(1)} %get-tuple-element.9.own_ref, bf16[8,32,1152]{2,1,0:T(8,128)(2,1)S(1)} %collective-permute-done.got_ref), custom_call_target="tpu_custom_call" | custom-call | tf_op jit(solution)/shard_map/pallas_call | solution.py:188
  79.3 0.0 copy-start.1
  79.3 13.5 %all_to_all.17.mine_ref = bf16[16,32,640]{2,1,0:T(8,128)(2,1)S(1)} all-to-all(bf16[16,32,640]{2,1,0:T(8,128)(2,1)S(1)} %bitcast.8), channel_id=1, replica_groups=mesh['zl'=8,'core'=2,'y'=4,'x'=4,'zh'=2] {'y','x'}, dimensions={0} | all-to-all | bytes 1310720 | tf_op jit(solution)/shard_map/all_to_all | solution.py:203
  92.8 5.2 %collective-permute-start.1 = (bf16[16,32,640]{2,1,0:T(8,128)(2,1)S(1)}, bf16[16,32,640]{2,1,0:T(8,128)(2,1)S(1)}, u32[]{:S(2)}, u32[]{:S(2)}) collective-permute-start(bf16[16,32,640]{2,1,0:T(8,128)(2,1)S(1)} %all_to_all.17.mine_ref), channel_id=1, source_target_pairs={{0,32},{32,0},{1,33},{33,1},{2,34},{34,2},{3,35},{35,3},{4,36},{36... | collective-permute-start | bytes 1966088 | tf_op jit(solution)/shard_map/ppermute | solution.py:227
  97.9 1.7 %collective-permute-done.1.other_ref = bf16[16,32,640]{2,1,0:T(8,128)(2,1)S(1)} collective-permute-done((bf16[16,32,640]{2,1,0:T(8,128)(2,1)S(1)}, bf16[16,32,640]{2,1,0:T(8,128)(2,1)S(1)}, u32[]{:S(2)}, u32[]{:S(2)}) %collective-permute-start.1) | collective-permute-done | bytes 655392 | tf_op jit(solution)/shard_map/ppermute | solution.py:227
  99.6 0.0 copy-done.1
  99.6 3.2 %shard_map.60 = f32[64,200]{1,0:T(8,128)} custom-call(f32[64,200]{1,0:T(8,128)S(1)} %bitcast.11, bf16[16,32,640]{2,1,0:T(8,128)(2,1)S(1)} %all_to_all.17.mine_ref, bf16[16,32,640]{2,1,0:T(8,128)(2,1)S(1)} %collective-permute-done.1.other_ref, bf16[1024,256]{1,0:T(8,128)(2,1)S(1)} %get-tuple-element.12.first_ref), custom_call_target="tpu_custom_call" | custom-call | tf_op jit(solution)/shard_map/pallas_call | solution.py:188
  (1 shorter events, 0.0 us)
Async XLA Ops:
  37.7 11.0 %copy-start = (bf16[1,200,1024]{2,1,0:T(8,128)(2,1)S(1)}, bf16[1,200,1024]{2,1,0:T(8,128)(2,1)}, u32[]{:S(2)}) copy-start(bf16[1,200,1024]{2,1,0:T(8,128)(2,1)} %param.7) | copy-start | bytes 1228804
  37.7 11.0 %copy-start.2 = (f32[1,200,200]{2,1,0:T(8,128)S(1)}, f32[1,200,200]{2,1,0:T(8,128)}, u32[]{:S(2)}) copy-start(f32[1,200,200]{2,1,0:T(8,128)} %param.6) | copy-start | bytes 480004
  37.9 10.9 %collective-permute-start = (bf16[8,32,1152]{2,1,0:T(8,128)(2,1)S(1)}, bf16[8,32,1152]{2,1,0:T(8,128)(2,1)S(1)}, u32[]{:S(2)}, u32[]{:S(2)}) collective-permute-start(bf16[8,32,1152]{2,1,0:T(8,128)(2,1)S(1)} %get-tuple-element.10), channel_id=1, source_target_pairs={{0,32},{32,0},{1,33},{33,1},{2,34},{34,2},{3,35},{35,3},{4,36},{36... | collective-permute-start | bytes 1769480 | tf_op jit(solution)/shard_map/ppermute | solution.py:216
  79.3 20.4 %copy-start.1 = (f32[1,64,200]{2,1,0:T(8,128)S(1)}, f32[1,64,200]{2,1,0:T(8,128)}, u32[]{:S(2)}) copy-start(f32[1,64,200]{2,1,0:T(8,128)} %param.5) | copy-start | bytes 153604
  92.8 6.9 %collective-permute-start.1 = (bf16[16,32,640]{2,1,0:T(8,128)(2,1)S(1)}, bf16[16,32,640]{2,1,0:T(8,128)(2,1)S(1)}, u32[]{:S(2)}, u32[]{:S(2)}) collective-permute-start(bf16[16,32,640]{2,1,0:T(8,128)(2,1)S(1)} %all_to_all.17.mine_ref), channel_id=1, source_target_pairs={{0,32},{32,0},{1,33},{33,1},{2,34},{34,2},{3,35},{35,3},{4,36},{36... | collective-permute-start | bytes 1966088 | tf_op jit(solution)/shard_map/ppermute | solution.py:227

commit v7 on v6

--- a/solution.py
+++ b/solution.py
@@ -115,11 +115,11 @@
     by_walker = jnp.concatenate([in_ref[:, 0, :], jnp.zeros((112, 128), f32)], axis=0)
     high = by_walker.astype(bf16)
     rest = (by_walker - high.astype(f32)).astype(bf16)
-    g, q = iota((128, 512), 0), iota((128, 512), 1) >> 5
+    g, q = iota((128, 256), 0), iota((128, 256), 1) >> 4
     vector = 2 * (q & 7) + jnp.where(q < 8, k, 1 - k)
     pick = jnp.where(g == vector, 1.0, 0.0).astype(bf16)
-    walkers = jnp.where((iota((512, 128), 0) >> 5) == iota((512, 128), 1), 1.0, 0.0).astype(bf16)
-    same = (iota((512, 512), 0) & 31) == (iota((512, 512), 1) & 31)
+    walkers = jnp.where((iota((256, 128), 0) >> 4) == iota((256, 128), 1), 1.0, 0.0).astype(bf16)
+    same = (iota((256, 256), 0) & 15) == (iota((256, 256), 1) & 15)
 
     def weights(part):
         spread = jnp.dot(part, pick, preferred_element_type=f32).astype(bf16)
@@ -127,14 +127,14 @@
         return jnp.where(same, full, 0.0).astype(bf16)
 
     w_high, w_rest = weights(high), weights(rest)
-    own = own_ref[:, :, 0:640].reshape(256, 640)
-    got = got_ref[:, :, 0:640].reshape(256, 640)
-    vectors = jnp.concatenate([own, got], axis=0)
     for i in range(2):
-        rows = slice(256 * i, 256 * i + 256)
-        value = jnp.dot(w_rest[rows], vectors, preferred_element_type=f32)
-        value += jnp.dot(w_high[rows], vectors, preferred_element_type=f32)
-        out_ref[rows, :] = value.astype(bf16)
+        rows = slice(16 * i, 16 * i + 16)
+        own = own_ref[:, rows, 0:640].reshape(128, 640)
+        got = got_ref[:, rows, 0:640].reshape(128, 640)
+        vectors = jnp.concatenate([own, got], axis=0)
+        value = jnp.dot(w_rest, vectors, preferred_element_type=f32)
+        value += jnp.dot(w_high, vectors, preferred_element_type=f32)
+        out_ref[:, rows, :] = value.astype(bf16).reshape(16, 16, 640)
 
 
 def taylor_kernel(orb_ref, mine_ref, other_ref, first_ref, out_ref, op, tail):
@@ -222,8 +222,8 @@
     along_z = exchange(partial, CHOL)
     summed = call(sum_kernel, shape((16, 1, 128), f32), along_z)
     everywhere = exchange(summed, PLANE)
-    pieces = call(operator_kernel, shape((512, 640), bf16), everywhere, own, got)
-    mine = exchange(pieces.reshape(16, 32, 640), PLANE)
+    pieces = call(operator_kernel, shape((16, 32, 640), bf16), everywhere, own, got)
+    mine = exchange(pieces, PLANE)
     other = lax.ppermute(mine, "core", swap_core)
     out = call(
         taylor_kernel, shape((64, 200), f32), orb, mine, other, first,

time: 103 us -> 102 us (level)
  no operation moved by 1% of the time
where the time goes in v7:
time: 102 us
  blocking collectives  77.3 us (76%)
  starting transfers between devices  14.4 us (14%)
  Pallas kernels  7.03 us (7%)
  waiting for transfers between devices  2.66 us (3%)
    all_to_all x3, blocking collectives, exchange(): return lax.all_to_all(value, axes, 0, 0, tiled=True)  41.2 us
    all_gather x1, blocking collectives, shards(): ring = lax.all_gather(packed, RING, axis=0, tiled=True)  36.1 us
    ppermute x1, starting transfers between devices, shards(): got = lax.ppermute(send, 'core', swap_core)  9.24 us
    pallas_call x6, Pallas kernels, call(): pl.pallas_call(body, out_shape=outs, in_specs=specs, out_specs=[vmem] * l...  7.03 us
    ppermute x1, starting transfers between devices, shards(): other = lax.ppermute(mine, 'core', swap_core)  5.16 us
  transfers between devices with their start and end apart: 2, of which 2 were waited for; matrix products, arithmetic and copies ran while one was open for 0% of the time, Pallas kernels for 0%

profile of v7, /device:TPU:1, one launch (start us, length us, event | category | flops | bytes accessed | tf_op | source)
XLA Modules:
  0.0 102.1 jit_solution(1215791115849184408)
XLA Ops:
  0.0 1.6 %shard_map.55 = bf16[32,976]{1,0:T(8,128)(2,1)} custom-call(f32[64,200]{1,0:T(8,128)} %bitcast.8, bf16[32,1024]{1,0:T(8,128)(2,1)} %bitcast.11), custom_call_target="tpu_custom_call" | custom-call | tf_op jit(solution)/shard_map/pallas_call | solution.py:188
  1.7 36.1 %all_gather.3 = bf16[512,976]{1,0:T(8,128)(2,1)S(1)} all-gather(bf16[32,976]{1,0:T(8,128)(2,1)} %shard_map.55), channel_id=1, replica_groups=mesh['zl'=8,'core'=2,'y'=4,'x'=4,'zh'=2] {'zh','zl'}, dimensions={0}, use_global_device_ids=true | all-gather | bytes 1061888 | tf_op jit(solution)/shard_map/all_gather | solution.py:213
  37.7 0.0 copy-start
  37.7 0.0 copy-start.2
  37.7 0.2 shard_map.56
  37.9 9.2 %collective-permute-start = (bf16[8,32,1152]{2,1,0:T(8,128)(2,1)S(1)}, bf16[8,32,1152]{2,1,0:T(8,128)(2,1)S(1)}, u32[]{:S(2)}, u32[]{:S(2)}) collective-permute-start(bf16[8,32,1152]{2,1,0:T(8,128)(2,1)S(1)} %get-tuple-element.10), channel_id=1, source_target_pairs={{0,32},{32,0},{1,33},{33,1},{2,34},{34,2},{3,35},{35,3},{4,36},{36... | collective-permute-start | bytes 1769480 | tf_op jit(solution)/shard_map/ppermute | solution.py:216
  47.8 1.0 collective-permute-done.got_ref
  48.8 0.0 copy-done
  48.8 0.0 copy-done.2
  48.8 1.1 %shard_map.57 = (bf16[1024,256]{1,0:T(8,128)(2,1)S(1)}, f32[16,1,128]{2,1,0:T(1,128)S(1)}) custom-call(f32[1,1]{1,0:T(1,128)S(6)} %copy.6.field_ref, bf16[8,32,1152]{2,1,0:T(8,128)(2,1)S(1)} %get-tuple-element.9.own_ref, bf16[8,32,1152]{2,1,0:T(8,128)(2,1)S(1)} %collective-permute-done.got_ref, f32[200,200]{1,0:T(8,128)S(1)} %bitcast.10, ...), custom_call_target="tpu_custom_call" | custom-call | tf_op jit(solution)/shard_map/pallas_call | solution.py:188
  49.9 14.8 %all_to_all.15.in_ref = f32[16,1,128]{2,1,0:T(1,128)S(1)} all-to-all(f32[16,1,128]{2,1,0:T(1,128)S(1)} %get-tuple-element.11), channel_id=1, replica_groups=mesh['zl'=8,'core'=2,'y'=4,'x'=4,'zh'=2] {'zl','core'}, dimensions={0} | all-to-all | bytes 16384 | tf_op jit(solution)/shard_map/all_to_all | solution.py:203
  64.7 13.0 %all_to_all.16.in_ref = f32[16,1,128]{2,1,0:T(1,128)S(1)} all-to-all(f32[16,1,128]{2,1,0:T(1,128)S(1)} %shard_map.58), channel_id=1, replica_groups=mesh['zl'=8,'core'=2,'y'=4,'x'=4,'zh'=2] {'y','x'}, dimensions={0} | all-to-all | bytes 16384 | tf_op jit(solution)/shard_map/all_to_all | solution.py:203
  77.7 0.8 shard_map.59
  78.5 0.0 copy-start.1
  78.5 13.5 %all_to_all.17.mine_ref = bf16[16,32,640]{2,1,0:T(8,128)(2,1)S(1)} all-to-all(bf16[16,32,640]{2,1,0:T(8,128)(2,1)S(1)} %shard_map.59), channel_id=1, replica_groups=mesh['zl'=8,'core'=2,'y'=4,'x'=4,'zh'=2] {'y','x'}, dimensions={0} | all-to-all | bytes 1310720 | tf_op jit(solution)/shard_map/all_to_all | solution.py:203
  92.0 5.2 %collective-permute-start.1 = (bf16[16,32,640]{2,1,0:T(8,128)(2,1)S(1)}, bf16[16,32,640]{2,1,0:T(8,128)(2,1)S(1)}, u32[]{:S(2)}, u32[]{:S(2)}) collective-permute-start(bf16[16,32,640]{2,1,0:T(8,128)(2,1)S(1)} %all_to_all.17.mine_ref), channel_id=1, source_target_pairs={{0,32},{32,0},{1,33},{33,1},{2,34},{34,2},{3,35},{35,3},{4,36},{36... | collective-permute-start | bytes 1966088 | tf_op jit(solution)/shard_map/ppermute | solution.py:227
  97.2 1.7 %collective-permute-done.1.other_ref = bf16[16,32,640]{2,1,0:T(8,128)(2,1)S(1)} collective-permute-done((bf16[16,32,640]{2,1,0:T(8,128)(2,1)S(1)}, bf16[16,32,640]{2,1,0:T(8,128)(2,1)S(1)}, u32[]{:S(2)}, u32[]{:S(2)}) %collective-permute-start.1) | collective-permute-done | bytes 655392 | tf_op jit(solution)/shard_map/ppermute | solution.py:227
  98.9 0.0 copy-done.1
  98.9 3.2 %shard_map.60 = f32[64,200]{1,0:T(8,128)} custom-call(f32[64,200]{1,0:T(8,128)S(1)} %bitcast.9, bf16[16,32,640]{2,1,0:T(8,128)(2,1)S(1)} %all_to_all.17.mine_ref, bf16[16,32,640]{2,1,0:T(8,128)(2,1)S(1)} %collective-permute-done.1.other_ref, bf16[1024,256]{1,0:T(8,128)(2,1)S(1)} %get-tuple-element.12.first_ref), custom_call_target="tpu_custom_call" | custom-call | tf_op jit(solution)/shard_map/pallas_call | solution.py:188
  (1 shorter events, 0.0 us)
Async XLA Ops:
  37.7 11.0 %copy-start = (bf16[1,200,1024]{2,1,0:T(8,128)(2,1)S(1)}, bf16[1,200,1024]{2,1,0:T(8,128)(2,1)}, u32[]{:S(2)}) copy-start(bf16[1,200,1024]{2,1,0:T(8,128)(2,1)} %param.7) | copy-start | bytes 1228804
  37.7 11.0 %copy-start.2 = (f32[1,200,200]{2,1,0:T(8,128)S(1)}, f32[1,200,200]{2,1,0:T(8,128)}, u32[]{:S(2)}) copy-start(f32[1,200,200]{2,1,0:T(8,128)} %param.6) | copy-start | bytes 480004
  37.9 10.9 %collective-permute-start = (bf16[8,32,1152]{2,1,0:T(8,128)(2,1)S(1)}, bf16[8,32,1152]{2,1,0:T(8,128)(2,1)S(1)}, u32[]{:S(2)}, u32[]{:S(2)}) collective-permute-start(bf16[8,32,1152]{2,1,0:T(8,128)(2,1)S(1)} %get-tuple-element.10), channel_id=1, source_target_pairs={{0,32},{32,0},{1,33},{33,1},{2,34},{34,2},{3,35},{35,3},{4,36},{36... | collective-permute-start | bytes 1769480 | tf_op jit(solution)/shard_map/ppermute | solution.py:216
  78.5 20.4 %copy-start.1 = (f32[1,64,200]{2,1,0:T(8,128)S(1)}, f32[1,64,200]{2,1,0:T(8,128)}, u32[]{:S(2)}) copy-start(f32[1,64,200]{2,1,0:T(8,128)} %param.5) | copy-start | bytes 153604
  92.0 6.9 %collective-permute-start.1 = (bf16[16,32,640]{2,1,0:T(8,128)(2,1)S(1)}, bf16[16,32,640]{2,1,0:T(8,128)(2,1)S(1)}, u32[]{:S(2)}, u32[]{:S(2)}) collective-permute-start(bf16[16,32,640]{2,1,0:T(8,128)(2,1)S(1)} %all_to_all.17.mine_ref), channel_id=1, source_target_pairs={{0,32},{32,0},{1,33},{33,1},{2,34},{34,2},{3,35},{35,3},{4,36},{36... | collective-permute-start | bytes 1966088 | tf_op jit(solution)/shard_map/ppermute | solution.py:227

commit v8 on v7

--- a/solution.py
+++ b/solution.py
@@ -137,16 +137,22 @@
         out_ref[:, rows, :] = value.astype(bf16).reshape(16, 16, 640)
 
 
-def taylor_kernel(orb_ref, mine_ref, other_ref, first_ref, out_ref, op, tail):
-    k = lax.axis_index("core")
+def place_rows(source, core, op, tail):
     for p in range(16):
-        here = pl.multiple_of(64 * p + 32 * k, 32)
-        there = pl.multiple_of(64 * p + 32 * (1 - k), 32)
-        for row, source in ((here, mine_ref), (there, other_ref)):
-            for d in range(4):
-                col = ((p // 2 + d) % 8) * 128
-                op[pl.ds(row, 32), col:col + 128] = source[p, :, 128 * d:128 * d + 128]
-            tail[pl.ds(row, 32), :] = source[p, :, 512:640].astype(f32)
+        row = pl.multiple_of(64 * p + 32 * core, 32)
+        for d in range(4):
+            col = ((p // 2 + d) % 8) * 128
+            op[pl.ds(row, 32), col:col + 128] = source[p, :, 128 * d:128 * d + 128]
+        tail[pl.ds(row, 32), :] = source[p, :, 512:640].astype(f32)
+
+
+def place_kernel(mine_ref, op, tail):
+    place_rows(mine_ref, lax.axis_index("core"), op, tail)
+
+
+def taylor_kernel(orb_ref, other_ref, first_ref, op_in, tail_in, out_ref, op, tail):
+    del op_in, tail_in
+    place_rows(other_ref, 1 - lax.axis_index("core"), op, tail)
     for i in range(8):
         for d in range(1, 4):
             j = (i + d) % 8
@@ -179,7 +185,7 @@
     out_ref[...] = orb_ref[...] + total[:, :200]
 
 
-def call(body, outs, *args, scratch=(), smem=0, hbm=(), grant=40):
+def call(body, outs, *args, scratch=(), smem=0, hbm=(), grant=40, aliases=None):
     vmem = pl.BlockSpec(memory_space=pltpu.VMEM)
     specs = [pl.BlockSpec(memory_space=pltpu.SMEM)] * smem + [vmem] * (len(args) - smem)
     for i in hbm:
@@ -191,6 +197,7 @@
         in_specs=specs,
         out_specs=[vmem] * len(outs) if many else vmem,
         scratch_shapes=list(scratch),
+        input_output_aliases=aliases or {},
         compiler_params=pltpu.CompilerParams(vmem_limit_bytes=grant * 2**20),
     )(*args)
 
@@ -225,9 +232,10 @@
     pieces = call(operator_kernel, shape((16, 32, 640), bf16), everywhere, own, got)
     mine = exchange(pieces, PLANE)
     other = lax.ppermute(mine, "core", swap_core)
-    out = call(
-        taylor_kernel, shape((64, 200), f32), orb, mine, other, first,
-        scratch=[pltpu.VMEM((1024, 1024), bf16), pltpu.VMEM((1024, 128), f32)],
+    halves = [shape((1024, 1024), bf16), shape((1024, 128), f32)]
+    op, tail = call(place_kernel, halves, mine)
+    out, _, _ = call(
+        taylor_kernel, [shape((64, 200), f32)] + halves, orb, other, first, op, tail, aliases={3: 1, 4: 2},
     )
     return out[None]
 

time: 102 us -> 102 us (level)
    pallas_call x6 -> x7, Pallas kernels: 7.03 us -> 7.08 us  [call(): pl.pallas_call(body, out_shape=outs, in_specs=specs, out_specs=[vmem] * l...]
where the time goes in v8:
time: 102 us
  blocking collectives  77.3 us (76%)
  starting transfers between devices  14.3 us (14%)
  Pallas kernels  7.08 us (7%)
  waiting for transfers between devices  2.55 us (2%)
    all_to_all x3, blocking collectives, exchange(): return lax.all_to_all(value, axes, 0, 0, tiled=True)  41.2 us
    all_gather x1, blocking collectives, shards(): ring = lax.all_gather(packed, RING, axis=0, tiled=True)  36.1 us
    ppermute x1, starting transfers between devices, shards(): got = lax.ppermute(send, 'core', swap_core)  9.11 us
    pallas_call x7, Pallas kernels, call(): pl.pallas_call(body, out_shape=outs, in_specs=specs, out_specs=[vmem] * l...  7.08 us
    ppermute x1, starting transfers between devices, shards(): other = lax.ppermute(mine, 'core', swap_core)  5.15 us
  transfers between devices with their start and end apart: 2, of which 2 were waited for; matrix products, arithmetic and copies ran while one was open for 0% of the time, Pallas kernels for 0%

profile of v8, /device:TPU:1, one launch (start us, length us, event | category | flops | bytes accessed | tf_op | source)
XLA Modules:
  0.0 101.9 jit_solution(12734002471177158920)
XLA Ops:
  0.0 0.0 copy-start
  0.0 0.0 copy-start.2
  0.0 1.7 %shard_map.55 = bf16[32,976]{1,0:T(8,128)(2,1)} custom-call(f32[64,200]{1,0:T(8,128)} %bitcast.8, bf16[32,1024]{1,0:T(8,128)(2,1)} %bitcast.11), custom_call_target="tpu_custom_call" | custom-call | tf_op jit(solution)/shard_map/pallas_call | solution.py:194
  1.7 36.1 %all_gather.3 = bf16[512,976]{1,0:T(8,128)(2,1)S(1)} all-gather(bf16[32,976]{1,0:T(8,128)(2,1)} %shard_map.55), channel_id=1, replica_groups=mesh['zl'=8,'core'=2,'y'=4,'x'=4,'zh'=2] {'zh','zl'}, dimensions={0}, use_global_device_ids=true | all-gather | bytes 1061888 | tf_op jit(solution)/shard_map/all_gather | solution.py:220
  37.8 0.2 shard_map.56
  38.0 9.1 %collective-permute-start = (bf16[8,32,1152]{2,1,0:T(8,128)(2,1)S(1)}, bf16[8,32,1152]{2,1,0:T(8,128)(2,1)S(1)}, u32[]{:S(2)}, u32[]{:S(2)}) collective-permute-start(bf16[8,32,1152]{2,1,0:T(8,128)(2,1)S(1)} %get-tuple-element.13), channel_id=1, source_target_pairs={{0,32},{32,0},{1,33},{33,1},{2,34},{34,2},{3,35},{35,3},{4,36},{36... | collective-permute-start | bytes 1769480 | tf_op jit(solution)/shard_map/ppermute | solution.py:223
  47.7 1.0 collective-permute-done.got_ref
  48.7 0.0 copy-done
  48.7 0.0 copy-done.2
  48.7 1.1 %shard_map.57 = (bf16[1024,256]{1,0:T(8,128)(2,1)S(1)}, f32[16,1,128]{2,1,0:T(1,128)S(1)}) custom-call(f32[1,1]{1,0:T(1,128)S(6)} %copy.10.field_ref, bf16[8,32,1152]{2,1,0:T(8,128)(2,1)S(1)} %get-tuple-element.12.own_ref, bf16[8,32,1152]{2,1,0:T(8,128)(2,1)S(1)} %collective-permute-done.got_ref, f32[200,200]{1,0:T(8,128)S(1)} %bitcast.10, ...), custom_call_target="tpu_custom_call" | custom-call | tf_op jit(solution)/shard_map/pallas_call | solution.py:194
  49.8 0.0 copy-start.1
  49.8 14.9 %all_to_all.15.in_ref = f32[16,1,128]{2,1,0:T(1,128)S(1)} all-to-all(f32[16,1,128]{2,1,0:T(1,128)S(1)} %get-tuple-element.14), channel_id=1, replica_groups=mesh['zl'=8,'core'=2,'y'=4,'x'=4,'zh'=2] {'zl','core'}, dimensions={0} | all-to-all | bytes 16384 | tf_op jit(solution)/shard_map/all_to_all | solution.py:210
  64.8 13.0 %all_to_all.16.in_ref = f32[16,1,128]{2,1,0:T(1,128)S(1)} all-to-all(f32[16,1,128]{2,1,0:T(1,128)S(1)} %shard_map.58), channel_id=1, replica_groups=mesh['zl'=8,'core'=2,'y'=4,'x'=4,'zh'=2] {'y','x'}, dimensions={0} | all-to-all | bytes 16384 | tf_op jit(solution)/shard_map/all_to_all | solution.py:210
  77.7 0.9 shard_map.59
  78.6 13.3 %all_to_all.17.mine_ref = bf16[16,32,640]{2,1,0:T(8,128)(2,1)S(1)} all-to-all(bf16[16,32,640]{2,1,0:T(8,128)(2,1)S(1)} %shard_map.59), channel_id=1, replica_groups=mesh['zl'=8,'core'=2,'y'=4,'x'=4,'zh'=2] {'y','x'}, dimensions={0} | all-to-all | bytes 1310720 | tf_op jit(solution)/shard_map/all_to_all | solution.py:210
  91.9 5.1 %collective-permute-start.1 = (bf16[16,32,640]{2,1,0:T(8,128)(2,1)S(1)}, bf16[16,32,640]{2,1,0:T(8,128)(2,1)S(1)}, u32[]{:S(2)}, u32[]{:S(2)}) collective-permute-start(bf16[16,32,640]{2,1,0:T(8,128)(2,1)S(1)} %all_to_all.17.mine_ref), channel_id=1, source_target_pairs={{0,32},{32,0},{1,33},{33,1},{2,34},{34,2},{3,35},{35,3},{4,36},{36... | collective-permute-start | bytes 1966088 | tf_op jit(solution)/shard_map/ppermute | solution.py:234
  97.1 0.1 shard_map.60
  97.2 1.6 %collective-permute-done.1.other_ref = bf16[16,32,640]{2,1,0:T(8,128)(2,1)S(1)} collective-permute-done((bf16[16,32,640]{2,1,0:T(8,128)(2,1)S(1)}, bf16[16,32,640]{2,1,0:T(8,128)(2,1)S(1)}, u32[]{:S(2)}, u32[]{:S(2)}) %collective-permute-start.1) | collective-permute-done | bytes 655392 | tf_op jit(solution)/shard_map/ppermute | solution.py:234
  98.8 0.0 copy-done.1
  98.8 3.1 %shard_map.61 = (f32[64,200]{1,0:T(8,128)}, bf16[1024,1024]{1,0:T(8,128)(2,1)S(1)}, f32[1024,128]{1,0:T(8,128)S(1)}) custom-call(f32[64,200]{1,0:T(8,128)S(1)} %bitcast.9, bf16[16,32,640]{2,1,0:T(8,128)(2,1)S(1)} %collective-permute-done.1.other_ref, ...), custom_call_target="tpu_custom_call", output_to_operand_aliasing={{1}: (3, {}), {2}: (4, {})} | custom-call | tf_op jit(solution)/shard_map/pallas_call | solution.py:194
  (1 shorter events, 0.0 us)
Async XLA Ops:
  0.0 48.7 %copy-start = (bf16[1,200,1024]{2,1,0:T(8,128)(2,1)S(1)}, bf16[1,200,1024]{2,1,0:T(8,128)(2,1)}, u32[]{:S(2)}) copy-start(bf16[1,200,1024]{2,1,0:T(8,128)(2,1)} %param.7) | copy-start | bytes 1228804
  0.0 48.7 %copy-start.2 = (f32[1,200,200]{2,1,0:T(8,128)S(1)}, f32[1,200,200]{2,1,0:T(8,128)}, u32[]{:S(2)}) copy-start(f32[1,200,200]{2,1,0:T(8,128)} %param.6) | copy-start | bytes 480004
  38.0 10.7 %collective-permute-start = (bf16[8,32,1152]{2,1,0:T(8,128)(2,1)S(1)}, bf16[8,32,1152]{2,1,0:T(8,128)(2,1)S(1)}, u32[]{:S(2)}, u32[]{:S(2)}) collective-permute-start(bf16[8,32,1152]{2,1,0:T(8,128)(2,1)S(1)} %get-tuple-element.13), channel_id=1, source_target_pairs={{0,32},{32,0},{1,33},{33,1},{2,34},{34,2},{3,35},{35,3},{4,36},{36... | collective-permute-start | bytes 1769480 | tf_op jit(solution)/shard_map/ppermute | solution.py:223
  49.8 49.0 %copy-start.1 = (f32[1,64,200]{2,1,0:T(8,128)S(1)}, f32[1,64,200]{2,1,0:T(8,128)}, u32[]{:S(2)}) copy-start(f32[1,64,200]{2,1,0:T(8,128)} %param.5) | copy-start | bytes 153604
  91.9 6.9 %collective-permute-start.1 = (bf16[16,32,640]{2,1,0:T(8,128)(2,1)S(1)}, bf16[16,32,640]{2,1,0:T(8,128)(2,1)S(1)}, u32[]{:S(2)}, u32[]{:S(2)}) collective-permute-start(bf16[16,32,640]{2,1,0:T(8,128)(2,1)S(1)} %all_to_all.17.mine_ref), channel_id=1, source_target_pairs={{0,32},{32,0},{1,33},{33,1},{2,34},{34,2},{3,35},{35,3},{4,36},{36... | collective-permute-start | bytes 1966088 | tf_op jit(solution)/shard_map/ppermute | solution.py:234

commit v9 on v8

--- a/solution.py
+++ b/solution.py
@@ -156,8 +156,7 @@
     for i in range(8):
         for d in range(1, 4):
             j = (i + d) % 8
-            block = op[128 * i:128 * i + 128, 128 * j:128 * j + 128].astype(f32)
-            op[128 * j:128 * j + 128, 128 * i:128 * i + 128] = block.T.astype(bf16)
+            op[128 * j:128 * j + 128, 128 * i:128 * i + 128] = op[128 * i:128 * i + 128, 128 * j:128 * j + 128].T
     left = iota((64, 128), 1) < 64
     for i in range(4):
         j = i + 4

time: 102 us -> 102 us (level)
  no operation moved by 1% of the time
where the time goes in v9:
time: 102 us
  blocking collectives  77.3 us (76%)
  starting transfers between devices  14.3 us (14%)
  Pallas kernels  7.06 us (7%)
  waiting for transfers between devices  2.55 us (2%)
    all_to_all x3, blocking collectives, exchange(): return lax.all_to_all(value, axes, 0, 0, tiled=True)  41.2 us
    all_gather x1, blocking collectives, shards(): ring = lax.all_gather(packed, RING, axis=0, tiled=True)  36.1 us
    ppermute x1, starting transfers between devices, shards(): got = lax.ppermute(send, 'core', swap_core)  9.11 us
    pallas_call x7, Pallas kernels, call(): pl.pallas_call(body, out_shape=outs, in_specs=specs, out_specs=[vmem] * l...  7.06 us
    ppermute x1, starting transfers between devices, shards(): other = lax.ppermute(mine, 'core', swap_core)  5.15 us
  transfers between devices with their start and end apart: 2, of which 2 were waited for; matrix products, arithmetic and copies ran while one was open for 0% of the time, Pallas kernels for 0%

profile of v9, /device:TPU:1, one launch (start us, length us, event | category | flops | bytes accessed | tf_op | source)
XLA Modules:
  0.0 101.9 jit_solution(17617337965647566477)
XLA Ops:
  0.0 0.0 copy-start
  0.0 0.0 copy-start.2
  0.0 1.7 %shard_map.55 = bf16[32,976]{1,0:T(8,128)(2,1)} custom-call(f32[64,200]{1,0:T(8,128)} %bitcast.8, bf16[32,1024]{1,0:T(8,128)(2,1)} %bitcast.11), custom_call_target="tpu_custom_call" | custom-call | tf_op jit(solution)/shard_map/pallas_call | solution.py:193
  1.7 36.1 %all_gather.3 = bf16[512,976]{1,0:T(8,128)(2,1)S(1)} all-gather(bf16[32,976]{1,0:T(8,128)(2,1)} %shard_map.55), channel_id=1, replica_groups=mesh['zl'=8,'core'=2,'y'=4,'x'=4,'zh'=2] {'zh','zl'}, dimensions={0}, use_global_device_ids=true | all-gather | bytes 1061888 | tf_op jit(solution)/shard_map/all_gather | solution.py:219
  37.8 0.2 shard_map.56
  38.0 9.1 %collective-permute-start = (bf16[8,32,1152]{2,1,0:T(8,128)(2,1)S(1)}, bf16[8,32,1152]{2,1,0:T(8,128)(2,1)S(1)}, u32[]{:S(2)}, u32[]{:S(2)}) collective-permute-start(bf16[8,32,1152]{2,1,0:T(8,128)(2,1)S(1)} %get-tuple-element.13), channel_id=1, source_target_pairs={{0,32},{32,0},{1,33},{33,1},{2,34},{34,2},{3,35},{35,3},{4,36},{36... | collective-permute-start | bytes 1769480 | tf_op jit(solution)/shard_map/ppermute | solution.py:222
  47.7 1.0 collective-permute-done.got_ref
  48.7 0.0 copy-done
  48.7 0.0 copy-done.2
  48.7 1.1 %shard_map.57 = (bf16[1024,256]{1,0:T(8,128)(2,1)S(1)}, f32[16,1,128]{2,1,0:T(1,128)S(1)}) custom-call(f32[1,1]{1,0:T(1,128)S(6)} %copy.10.field_ref, bf16[8,32,1152]{2,1,0:T(8,128)(2,1)S(1)} %get-tuple-element.12.own_ref, bf16[8,32,1152]{2,1,0:T(8,128)(2,1)S(1)} %collective-permute-done.got_ref, f32[200,200]{1,0:T(8,128)S(1)} %bitcast.10, ...), custom_call_target="tpu_custom_call" | custom-call | tf_op jit(solution)/shard_map/pallas_call | solution.py:193
  49.8 0.0 copy-start.1
  49.8 14.9 %all_to_all.15.in_ref = f32[16,1,128]{2,1,0:T(1,128)S(1)} all-to-all(f32[16,1,128]{2,1,0:T(1,128)S(1)} %get-tuple-element.14), channel_id=1, replica_groups=mesh['zl'=8,'core'=2,'y'=4,'x'=4,'zh'=2] {'zl','core'}, dimensions={0} | all-to-all | bytes 16384 | tf_op jit(solution)/shard_map/all_to_all | solution.py:209
  64.8 13.0 %all_to_all.16.in_ref = f32[16,1,128]{2,1,0:T(1,128)S(1)} all-to-all(f32[16,1,128]{2,1,0:T(1,128)S(1)} %shard_map.58), channel_id=1, replica_groups=mesh['zl'=8,'core'=2,'y'=4,'x'=4,'zh'=2] {'y','x'}, dimensions={0} | all-to-all | bytes 16384 | tf_op jit(solution)/shard_map/all_to_all | solution.py:209
  77.7 0.9 shard_map.59
  78.6 13.3 %all_to_all.17.mine_ref = bf16[16,32,640]{2,1,0:T(8,128)(2,1)S(1)} all-to-all(bf16[16,32,640]{2,1,0:T(8,128)(2,1)S(1)} %shard_map.59), channel_id=1, replica_groups=mesh['zl'=8,'core'=2,'y'=4,'x'=4,'zh'=2] {'y','x'}, dimensions={0} | all-to-all | bytes 1310720 | tf_op jit(solution)/shard_map/all_to_all | solution.py:209
  91.9 5.1 %collective-permute-start.1 = (bf16[16,32,640]{2,1,0:T(8,128)(2,1)S(1)}, bf16[16,32,640]{2,1,0:T(8,128)(2,1)S(1)}, u32[]{:S(2)}, u32[]{:S(2)}) collective-permute-start(bf16[16,32,640]{2,1,0:T(8,128)(2,1)S(1)} %all_to_all.17.mine_ref), channel_id=1, source_target_pairs={{0,32},{32,0},{1,33},{33,1},{2,34},{34,2},{3,35},{35,3},{4,36},{36... | collective-permute-start | bytes 1966088 | tf_op jit(solution)/shard_map/ppermute | solution.py:233
  97.1 0.1 shard_map.60
  97.2 1.6 %collective-permute-done.1.other_ref = bf16[16,32,640]{2,1,0:T(8,128)(2,1)S(1)} collective-permute-done((bf16[16,32,640]{2,1,0:T(8,128)(2,1)S(1)}, bf16[16,32,640]{2,1,0:T(8,128)(2,1)S(1)}, u32[]{:S(2)}, u32[]{:S(2)}) %collective-permute-start.1) | collective-permute-done | bytes 655392 | tf_op jit(solution)/shard_map/ppermute | solution.py:233
  98.8 0.0 copy-done.1
  98.8 3.1 %shard_map.61 = (f32[64,200]{1,0:T(8,128)}, bf16[1024,1024]{1,0:T(8,128)(2,1)S(1)}, f32[1024,128]{1,0:T(8,128)S(1)}) custom-call(f32[64,200]{1,0:T(8,128)S(1)} %bitcast.9, bf16[16,32,640]{2,1,0:T(8,128)(2,1)S(1)} %collective-permute-done.1.other_ref, ...), custom_call_target="tpu_custom_call", output_to_operand_aliasing={{1}: (3, {}), {2}: (4, {})} | custom-call | tf_op jit(solution)/shard_map/pallas_call | solution.py:193
  (1 shorter events, 0.0 us)
Async XLA Ops:
  0.0 48.7 %copy-start = (bf16[1,200,1024]{2,1,0:T(8,128)(2,1)S(1)}, bf16[1,200,1024]{2,1,0:T(8,128)(2,1)}, u32[]{:S(2)}) copy-start(bf16[1,200,1024]{2,1,0:T(8,128)(2,1)} %param.7) | copy-start | bytes 1228804
  0.0 48.7 %copy-start.2 = (f32[1,200,200]{2,1,0:T(8,128)S(1)}, f32[1,200,200]{2,1,0:T(8,128)}, u32[]{:S(2)}) copy-start(f32[1,200,200]{2,1,0:T(8,128)} %param.6) | copy-start | bytes 480004
  38.0 10.7 %collective-permute-start = (bf16[8,32,1152]{2,1,0:T(8,128)(2,1)S(1)}, bf16[8,32,1152]{2,1,0:T(8,128)(2,1)S(1)}, u32[]{:S(2)}, u32[]{:S(2)}) collective-permute-start(bf16[8,32,1152]{2,1,0:T(8,128)(2,1)S(1)} %get-tuple-element.13), channel_id=1, source_target_pairs={{0,32},{32,0},{1,33},{33,1},{2,34},{34,2},{3,35},{35,3},{4,36},{36... | collective-permute-start | bytes 1769480 | tf_op jit(solution)/shard_map/ppermute | solution.py:222
  49.8 49.0 %copy-start.1 = (f32[1,64,200]{2,1,0:T(8,128)S(1)}, f32[1,64,200]{2,1,0:T(8,128)}, u32[]{:S(2)}) copy-start(f32[1,64,200]{2,1,0:T(8,128)} %param.5) | copy-start | bytes 153604
  91.9 6.9 %collective-permute-start.1 = (bf16[16,32,640]{2,1,0:T(8,128)(2,1)S(1)}, bf16[16,32,640]{2,1,0:T(8,128)(2,1)S(1)}, u32[]{:S(2)}, u32[]{:S(2)}) collective-permute-start(bf16[16,32,640]{2,1,0:T(8,128)(2,1)S(1)} %all_to_all.17.mine_ref), channel_id=1, source_target_pairs={{0,32},{32,0},{1,33},{33,1},{2,34},{34,2},{3,35},{35,3},{4,36},{36... | collective-permute-start | bytes 1966088 | tf_op jit(solution)/shard_map/ppermute | solution.py:233
